TPU v7x, 256 devices: a whole 4x4x8 slice. The times are simulated.
256 devices in a mesh: lat: 8 (over x, core), lon: 8 (over z), dep: 4 (over y).
Axes of the slice: x: 4, y: 4, z: 8, core: 2. Of those that a mesh axis runs over, the one named last changes fastest.
Arguments:
- kernels: bfloat16 [524288, 6, 128], P(('lat', 'lon', 'dep')), may hold values from -6 to 6
- basis_weights: bfloat16 [8, 128, 128], replicated, may hold values from -0.5 to 0.5
- owner_block: int32 [524288, 1], P(('lat', 'lon', 'dep')), may hold values from 0 to 63; in each aligned block of 2048 rows (0 to 2047, 2048 to 4095, ...) at most 64 rows name the same one
- column_offset: int32 [524288], P(('lat', 'lon', 'dep')), may hold values from 0 to 63
- basis_index: int32 [524288], P(('lat', 'lon', 'dep')), may hold values from 0 to 7
Outputs:
- projected: float32 [6, 64, 64, 512], P(None, 'lat', 'lon', 'dep')
- smoothed: float32 [6, 64, 64, 512], P(None, 'lat', 'lon', 'dep')
Inputs may be any that keep to these rules, and one draw needn't show every extreme that they name: `owner_block`: among the rows of one device, no block is named more than 64 times, and some block is named exactly 64 times.
All inputs are finite; a program needn't handle non-finite values.
Results may differ from a plain program's by a relative error of at most 0.0003.
Values sent between devices are 32-bit elements; how exact they have to be, the bound alone decides.
No kernel may reach another device: no remote copies, remote signals or barrier semaphores. Data moves between devices by JAX's collectives and lax.ppermute only.
A program may use at most 128 MiB of HBM per device.

v0:
```python
import math

import jax
import jax.numpy as jnp
from jax import lax
from jax.sharding import PartitionSpec as P

GX = 8
GY = 8
RADIUS = 4


def with_halo(block, sides, width):
    for axis, dim in sides:
        count = lax.axis_size(axis)
        forward = [(i, i + 1) for i in range(count - 1)]
        backward = [(target, source) for source, target in forward]
        low = lax.ppermute(
            lax.slice_in_dim(block, block.shape[dim] - width, None, axis=dim), axis, forward
        )
        high = lax.ppermute(lax.slice_in_dim(block, 0, width, axis=dim), axis, backward)
        block = jnp.concatenate([low, block, high], axis=dim)
    return block


def gauss_taps():
    weights = [math.exp(-(offset * offset) / 8.0) for offset in range(-RADIUS, RADIUS + 1)]
    total = 0.0
    for value in weights:
        total = total + value
    return [value / total for value in weights]


def pass_along(padded, axis_pos):
    length = padded.shape[axis_pos] - 2 * RADIUS
    result = None
    for place, factor in enumerate(gauss_taps()):
        term = factor * lax.slice_in_dim(padded, place, place + length, axis=axis_pos)
        result = term if result is None else result + term
    return result


def local(kernels, basis_weights, owner_block, column_offset, basis_index):
    elem_count, channels, point_count = kernels.shape
    basis_count, _, depth_cells = basis_weights.shape
    groups = lax.axis_size(("lat", "lon"))
    stacked = basis_weights.reshape(basis_count * point_count, depth_cells)
    block_len = min(256, elem_count)
    block_total = elem_count // block_len

    def project_block(inputs_pair):
        kernel_rows, chosen = inputs_pair
        picked = (chosen[:, None] == jnp.arange(basis_count, dtype=jnp.int32)[None, :]).astype(
            jnp.bfloat16
        )
        expanded = (kernel_rows[:, :, None, :] * picked[:, None, :, None]).reshape(
            block_len * channels, basis_count * point_count
        )
        result = jnp.dot(expanded, stacked, preferred_element_type=jnp.float32)
        return result.reshape(block_len, channels * depth_cells)

    contribution = lax.map(
        project_block,
        (
            kernels.reshape(block_total, block_len, channels, point_count),
            basis_index.reshape(block_total, block_len),
        ),
    )
    contribution = contribution.reshape(elem_count, channels * depth_cells)
    owners = owner_block[:, 0]
    tiles = GX * GY
    capacity = 2 * elem_count // groups
    owner_hits = (owners[:, None] == jnp.arange(groups, dtype=jnp.int32)[None, :]).astype(jnp.int32)
    slot_rank = jnp.sum(jnp.cumsum(owner_hits, 0) * owner_hits, 1) - 1
    outgoing = (
        jnp.zeros((groups, capacity, channels * depth_cells), jnp.float32)
        .at[owners, slot_rank]
        .set(contribution)
    )
    places = (
        jnp.full((groups, capacity), -1.0, jnp.float32)
        .at[owners, slot_rank]
        .set(column_offset.astype(jnp.float32))
    )
    arrived, arrived_places = (
        lax.all_to_all(outgoing, ("lat", "lon"), split_axis=0, concat_axis=0, tiled=True),
        lax.all_to_all(places, ("lat", "lon"), split_axis=0, concat_axis=0, tiled=True),
    )
    column_hit = (
        arrived_places.reshape(-1)[:, None] == jnp.arange(tiles, dtype=jnp.float32)[None, :]
    ).astype(jnp.float32)
    block = jnp.einsum(
        "rn,rk->nk",
        column_hit,
        arrived.reshape(-1, channels * depth_cells),
        precision=lax.Precision.HIGHEST,
    )
    projected = jnp.transpose(block.reshape(GX, GY, channels, depth_cells), (2, 0, 1, 3))
    along_lat = pass_along(with_halo(projected, (("lat", 1),), RADIUS), 1)
    along_lon = pass_along(with_halo(along_lat, (("lon", 2),), RADIUS), 2)
    smoothed = pass_along(with_halo(along_lon, (("dep", 3),), RADIUS), 3)
    return (projected, smoothed)


def solution(mesh):
    placed = (
        P(("lat", "lon", "dep"), None, None),
        P(),
        P(("lat", "lon", "dep"), None),
        P(("lat", "lon", "dep")),
        P(("lat", "lon", "dep")),
    )
    return jax.shard_map(
        local,
        mesh=mesh,
        in_specs=placed,
        out_specs=(P(None, "lat", "lon", "dep"), P(None, "lat", "lon", "dep")),
        check_vma=False,
    )
```

profile of v0, /device:TPU:1, one launch (start us, length us, event | category | flops | bytes accessed | tf_op | source)
XLA Modules:
  0.0 446.4 jit_solution(3497860029773820216)
XLA Ops:
  1.4 18.1 %reduce-window.6 = s32[64,16,128]{2,1,0:T(8,128)S(1)} reduce-window(s32[64,16,128]{2,1,0:T(8,128)S(1)} %fusion.12, s32[]{:T(128)} %copy.34), window={size=1x1x128 pad=0_0x0_0x127_0}, to_apply=%region_0.1 | reduce-window | flops 16646144 | bytes 1048580 | tf_op jit(solution)/shard_map/reduce-window
  23.8 8.1 %scatter_custom_fusion = f32[4096]{0:T(1024)S(1)} fusion(s32[2048]{0:T(1024)S(1)} %broadcast_select_fusion, f32[2048]{0:T(1024)S(1)} %convert_element_type.17, f32[]{:T(128)} %constant.11.clone.1), kind=kCustom, calls=%fused_computation.138 | custom fusion | bytes 16388
  32.5 13.0 %all-to-all-start = ((f32[64,1,64]{2,1,0:T(1,128)}), f32[64,1,64]{2,1,0:T(1,128)S(1)}, u32[]{:S(2)}, u32[]{:S(2)}) async-start(f32[64,1,64]{2,1,0:T(1,128)} %all_to_all.9), calls=%async_computation | async-start | bytes 65536 | tf_op jit(solution)/shard_map/all_to_all | solution.py:87
  45.5 5.5 %copy.12 = bf16[2048,6,128]{2,1,0:T(8,128)(2,1)} copy(bf16[2048,6,128]{2,0,1:T(8,128)(2,1)} %param.7) | data formatting | bytes 6291456 | tf_op args[0]
  51.1 31.7 %while.10 = (s32[]{:T(128)}, f32[8,256,768]{2,1,0:T(8,128)}, bf16[8,256,6,128]{3,2,1,0:T(8,128)(2,1)}, s32[8,256]{1,0:T(8,128)S(1)}, bf16[1024,128]{1,0:T(8,128)(2,1)S(1)}, /*index=5*/s32[]{:T(128)}) while((s32[]{:T(128)}, f32[8,256,768]{2,1,0:T(8,128)}, bf16[8,256,6,128]{3,2,1,0:T(8,128)(2,1)}, s32[8,256]{1,0:T(8,128)S(1)}, ...), condition=%wide.region_5.6_spmd, body=%wide.region_4.5_spmd.sunk | while | flops 404230144 | bytes 11677261 | solution.py:62
  51.1 1.1 dynamic-slice_bitcast_fusion.2
  55.0 1.1 dynamic-slice_bitcast_fusion.2
  59.0 1.1 dynamic-slice_bitcast_fusion.2
  63.0 1.1 dynamic-slice_bitcast_fusion.2
  82.8 15.1 %scatter_custom_fusion.1 = f32[4096,768]{1,0:T(8,128)} fusion(s32[2048]{0:T(1024)S(1)} %broadcast_select_fusion, f32[2048,768]{1,0:T(8,128)} %bitcast.69, f32[]{:T(128)} %constant.36.clone.1), kind=kCustom, calls=%fused_computation.11 | custom fusion | bytes 12583424
  97.9 10.5 %all-to-all-start.1 = ((f32[64,64,768]{2,1,0:T(8,128)}), f32[64,64,768]{2,1,0:T(8,128)}, u32[]{:S(2)}, u32[]{:S(2)}) async-start(f32[64,64,768]{2,1,0:T(8,128)} %bitcast.58), calls=%async_computation.1 | async-start | bytes 25165824 | tf_op jit(solution)/shard_map/all_to_all | solution.py:86
  109.7 275.8 %all-to-all-done.1 = f32[64,64,768]{2,1,0:T(8,128)} async-done(((f32[64,64,768]{2,1,0:T(8,128)}), f32[64,64,768]{2,1,0:T(8,128)}, u32[]{:S(2)}, u32[]{:S(2)}) %all-to-all-start.1) | async-done | bytes 12582944 | tf_op jit(solution)/shard_map/all_to_all | solution.py:86
  385.5 12.6 %copy.13 = f32[768,4096]{1,0:T(8,128)} copy(f32[768,4096]{0,1:T(8,128)} %bitcast.16) | data formatting | bytes 25165824 | tf_op jit(solution)/shard_map/rn,rk->nk/dot_general | solution.py:92
  398.1 9.7 %convolution_bitcast_fusion = f32[6,8,8,128]{3,2,0,1:T(8,128)S(1)} fusion(f32[6,128,4096,1]{2,1,0,3:T(8,128)} %bitcast.59, f32[8,8]{1,0:T(8,128)S(1)} %multiply_add_fusion, f32[4096]{0:T(1024)S(1)} %eq.83), kind=kOutput, calls=%fused_computation.13 | convolution fusion | flops 2416181248 | bytes 12796160 | tf_op jit(solution)/shard_map/rn,rk->nk/dot_general | solution.py:92
  407.8 10.1 %collective-permute-start = (f32[6,4,8,128]{3,2,0,1:T(8,128)S(1)}, f32[6,4,8,128]{3,2,0,1:T(8,128)S(1)}, u32[]{:S(2)}, u32[]{:S(2)}) collective-permute-start(f32[6,4,8,128]{3,2,0,1:T(8,128)S(1)} %get-tuple-element.48), channel_id=1, source_target_pairs={{0,32},{32,64},{64,96},{96,128},{128,160},{160,192},{192,224},{1,3... | collective-permute-start | bytes 294920 | tf_op jit(solution)/shard_map/ppermute | solution.py:18
  418.0 1.9 collective-permute-start.1
  419.9 4.0 collective-permute-done.1
  424.1 3.7 collective-permute-start.2
  427.7 1.3 collective-permute-start.3
  429.3 3.7 collective-permute-done.3
  433.6 3.2 collective-permute-start.4
  436.8 1.3 collective-permute-start.5
  438.8 2.0 collective-permute-done.4
  440.7 4.1 collective-permute-done.5
  (86 shorter events, 37.0 us)
Async XLA Ops:
  0.6 50.4 %copy-start = (s32[2048]{0:T(1024)S(1)}, s32[2048]{0:T(1024)}, u32[]{:S(2)}) copy-start(s32[2048]{0:T(1024)} %param.11) | copy-start | bytes 24580
  0.6 50.4 %copy-start.1 = (bf16[8,128,128]{2,1,0:T(8,128)(2,1)S(1)}, bf16[8,128,128]{2,1,0:T(8,128)(2,1)}, u32[]{:S(2)}) copy-start(bf16[8,128,128]{2,1,0:T(8,128)(2,1)} %param.8) | copy-start | bytes 786436
  32.5 65.4 %all-to-all-start = ((f32[64,1,64]{2,1,0:T(1,128)}), f32[64,1,64]{2,1,0:T(1,128)S(1)}, u32[]{:S(2)}, u32[]{:S(2)}) async-start(f32[64,1,64]{2,1,0:T(1,128)} %all_to_all.9), calls=%async_computation | async-start | bytes 65536 | tf_op jit(solution)/shard_map/all_to_all | solution.py:87
  97.9 287.6 %all-to-all-start.1 = ((f32[64,64,768]{2,1,0:T(8,128)}), f32[64,64,768]{2,1,0:T(8,128)}, u32[]{:S(2)}, u32[]{:S(2)}) async-start(f32[64,64,768]{2,1,0:T(8,128)} %bitcast.58), calls=%async_computation.1 | async-start | bytes 25165824 | tf_op jit(solution)/shard_map/all_to_all | solution.py:86
  407.8 12.1 %collective-permute-start = (f32[6,4,8,128]{3,2,0,1:T(8,128)S(1)}, f32[6,4,8,128]{3,2,0,1:T(8,128)S(1)}, u32[]{:S(2)}, u32[]{:S(2)}) collective-permute-start(f32[6,4,8,128]{3,2,0,1:T(8,128)S(1)} %get-tuple-element.48), channel_id=1, source_target_pairs={{0,32},{32,64},{64,96},{96,128},{128,160},{160,192},{192,224},{1,3... | collective-permute-start | bytes 294920 | tf_op jit(solution)/shard_map/ppermute | solution.py:18
  418.0 5.9 %collective-permute-start.1 = (f32[6,4,8,128]{3,2,0,1:T(8,128)S(1)}, f32[6,4,8,128]{3,2,0,1:T(8,128)S(1)}, u32[]{:S(2)}, u32[]{:S(2)}) collective-permute-start(f32[6,4,8,128]{3,2,0,1:T(8,128)S(1)} %get-tuple-element.49), channel_id=1, source_target_pairs={{32,0},{64,32},{96,64},{128,96},{160,128},{192,160},{224,192},{33,... | collective-permute-start | bytes 294920 | tf_op jit(solution)/shard_map/ppermute | solution.py:21
  424.1 5.3 %collective-permute-start.2 = (f32[6,8,4,128]{3,2,0,1:T(4,128)S(1)}, f32[6,8,4,128]{3,2,0,1:T(4,128)S(1)}, u32[]{:S(2)}, u32[]{:S(2)}) collective-permute-start(f32[6,8,4,128]{3,2,0,1:T(4,128)S(1)} %get-tuple-element.46), channel_id=1, source_target_pairs={{0,4},{4,8},{8,12},{12,16},{16,20},{20,24},{24,28},{1,5},{5,9},{9,... | collective-permute-start | bytes 294920 | tf_op jit(solution)/shard_map/ppermute | solution.py:18
  427.7 5.4 %collective-permute-start.3 = (f32[6,8,4,128]{3,2,0,1:T(4,128)S(1)}, f32[6,8,4,128]{3,2,0,1:T(4,128)S(1)}, u32[]{:S(2)}, u32[]{:S(2)}) collective-permute-start(f32[6,8,4,128]{3,2,0,1:T(4,128)S(1)} %get-tuple-element.47), channel_id=1, source_target_pairs={{4,0},{8,4},{12,8},{16,12},{20,16},{24,20},{28,24},{5,1},{9,5},{13... | collective-permute-start | bytes 294920 | tf_op jit(solution)/shard_map/ppermute | solution.py:21
  433.6 7.2 %collective-permute-start.4 = (f32[6,8,8,4]{3,2,0,1:T(8,128)S(1)}, f32[6,8,8,4]{3,2,0,1:T(8,128)S(1)}, u32[]{:S(2)}, u32[]{:S(2)}) collective-permute-start(f32[6,8,8,4]{3,2,0,1:T(8,128)S(1)} %get-tuple-element.44), channel_id=1, source_target_pairs={{0,1},{1,2},{2,3},{4,5},{5,6},{6,7},{8,9},{9,10},{10,11},{12,13},{... | collective-permute-start | bytes 18440 | tf_op jit(solution)/shard_map/ppermute | solution.py:18
  436.8 8.1 %collective-permute-start.5 = (f32[6,8,8,4]{3,2,0,1:T(8,128)S(1)}, f32[6,8,8,4]{3,2,0,1:T(8,128)S(1)}, u32[]{:S(2)}, u32[]{:S(2)}) collective-permute-start(f32[6,8,8,4]{3,2,0,1:T(8,128)S(1)} %get-tuple-element.45), channel_id=1, source_target_pairs={{1,0},{2,1},{3,2},{5,4},{6,5},{7,6},{9,8},{10,9},{11,10},{13,12},{... | collective-permute-start | bytes 18440 | tf_op jit(solution)/shard_map/ppermute | solution.py:21
where the time goes:
time: 447 us; the launch traced here: 446 us
  waiting for transfers between devices  290 us (65%)
  local copies, waits for them, and re-layouts  62.7 us (14%)
  starting transfers between devices  45 us (10%)
  other arithmetic  30.1 us (7%)
  matrix products  17.5 us (4%)
    all_to_all x1, waiting for transfers between devices, local(): lax.all_to_all(outgoing, ('lat', 'lon'), split_axis=0, concat_axis=0, til...  276 us
    unnamed x9, local copies, waits for them, and re-layouts  30 us
    another operation x3, other arithmetic  18.5 us
    ppermute x3, starting transfers between devices, with_halo(): lax.ppermute(lax.slice_in_dim(block, block.shape[dim] - width, None, axis...  17 us
    all_to_all x1, starting transfers between devices, local(): lax.all_to_all(places, ('lat', 'lon'), split_axis=0, concat_axis=0, tiled...  13 us
    dot_general x1, local copies, waits for them, and re-layouts, local(): jnp.einsum('rn,rk->nk', column_hit, arrived.reshape(-1, channels * depth_...  12.6 us
    ppermute x3, waiting for transfers between devices, with_halo(): lax.ppermute(lax.slice_in_dim(block, 0, width, axis=dim), axis, backward)  11.8 us
    all_to_all x1, starting transfers between devices, local(): lax.all_to_all(outgoing, ('lat', 'lon'), split_axis=0, concat_axis=0, til...  10.5 us
  transfers between devices with their start and end apart: 8, of which 6 were waited for; matrix products, arithmetic and copies ran while one was open for 12% of the time, Pallas kernels for 0%

commit v1 on v0

v1 whole, which is shorter than its diff:
```python
import functools
import math

import jax
import jax.numpy as jnp
import numpy as np
from jax import lax
from jax.experimental import pallas as pl
from jax.experimental.pallas import tpu as pltpu
from jax.sharding import PartitionSpec as P

GX = 8
GY = 8
RADIUS = 4
CHIPS = 4
LON = 8
CHUNK = 64
WIDTH = 32
UNROLL = 16

CORE = [(i, i ^ 1) for i in range(2 * CHIPS)]
RING_X = [(2 * x + c, 2 * ((x + 1 - 2 * c) % CHIPS) + c) for x in range(CHIPS) for c in range(2)]
RING_Z = [
    (lat * LON + z, lat * LON + (z + 1 - 2 * (lat % 2)) % LON)
    for lat in range(2 * CHIPS)
    for z in range(LON)
]

MINE_A = [(3, 0), (2, 0), (1, 0), (0, 1), (1, 1), (2, 1), (3, 1), (4, 1)]
THEIRS_A = [(5, 1), (6, 1), (7, 1), (0, 0), (7, 0), (6, 0), (5, 0), (4, 0)]
LAYOUT_A = (
    [(2, q, 1) for q in range(LON)]
    + [(1, q, own) for q, own in MINE_A + THEIRS_A]
    + [(0, q, own) for q, own in MINE_A]
)
MINE_B = [(1, 0), (0, 1), (1, 1), (2, 1)]
THEIRS_B = [(3, 1), (0, 0), (3, 0), (2, 0)]
LAYOUT_B = (
    [(p, 4, 1) for p in range(CHIPS)]
    + [(p, q, own) for q in (3, 2, 1) for p, own in MINE_B + THEIRS_B]
    + [(p, 0, own) for p, own in MINE_B]
)
PARTS_A = (8, 16, 8)
PARTS_B = (4, 8, 8, 8, 4)


def block_tables():
    table = np.zeros((2 * CHIPS, LON, 2, 2 * CHIPS * LON), np.int32)
    for lat in range(2 * CHIPS):
        for z in range(LON):
            for owner in range(2 * CHIPS * LON):
                core = owner // LON % 2
                dx = (owner // LON // 2 - lat // 2) % CHIPS
                dz = (owner % LON - z) % LON
                by_x = {0: None, 1: 0, 2: core, 3: 1}[dx]
                by_z = {0: None, 4: core}.get(dz, 0 if dz < 4 else 1)
                for half, (first, second, layout) in enumerate(
                    ((by_x, by_z, LAYOUT_A), (by_z, by_x, LAYOUT_B))
                ):
                    handler = first if first is not None else second if second is not None else core
                    sign = 1 - 2 * handler
                    place = layout.index((dx * sign % CHIPS, dz * sign % LON, int(core == handler)))
                    table[lat, z, half, owner] = (
                        half * 64 + (0 if handler == lat % 2 else 32) + place
                    )
    return table * (6 * WIDTH)


def project_kernel(
    sizes, kernels_ref, weights_ref, owner_ref, column_ref, basis_ref, table_ref, *rest
):
    outs = rest[: len(sizes)]
    pos_v, row_v, end_v, pos_s, row_s, end_s, stage, acc, sems, copy_sems = rest[len(sizes) :]
    rows, lanes = owner_ref.shape
    elems = rows * lanes
    basis_count = weights_ref.shape[0]
    channels = kernels_ref.shape[1]

    owner = owner_ref[...]
    column = column_ref[...]
    first = jnp.zeros((rows, lanes), jnp.int32)
    second = jnp.zeros((rows, lanes), jnp.int32)
    for o in range(table_ref.shape[1]):
        hit = owner == o
        first = jnp.where(hit, table_ref[0, o], first)
        second = jnp.where(hit, table_ref[1, o], second)
    row_v[...] = jnp.where(column < WIDTH, first + column, second + column - WIDTH)

    basis = basis_ref[...]
    upper = (
        lax.broadcasted_iota(jnp.int32, (lanes, lanes), 0)
        <= lax.broadcasted_iota(jnp.int32, (lanes, lanes), 1)
    ).astype(jnp.float32)
    lower = (
        lax.broadcasted_iota(jnp.int32, (rows, rows), 1)
        < lax.broadcasted_iota(jnp.int32, (rows, rows), 0)
    ).astype(jnp.float32)
    base = jnp.zeros((1, lanes), jnp.int32)
    pos = jnp.zeros((rows, lanes), jnp.int32)
    for b in range(basis_count):
        hit = basis == b
        inside = jnp.dot(hit.astype(jnp.float32), upper, preferred_element_type=jnp.float32)
        in_row = jnp.broadcast_to(inside[:, lanes - 1 :], (rows, lanes))
        before = jnp.dot(lower, in_row, preferred_element_type=jnp.float32)
        rank = (before + inside).astype(jnp.int32) - 1
        total = (before + in_row)[rows - 1 :].astype(jnp.int32)
        pos = jnp.where(hit, base + rank, pos)
        base = base + (total + CHUNK - 1) // CHUNK * CHUNK
        end_v[pl.ds(b, 1), :] = base // CHUNK
    pos_v[...] = pos
    loads = [
        pltpu.make_async_copy(pos_v, pos_s, sems.at[0]),
        pltpu.make_async_copy(row_v, row_s, sems.at[1]),
        pltpu.make_async_copy(end_v, end_s, sems.at[2]),
    ]
    for load in loads:
        load.start()

    def clear(i, _):
        acc[pl.ds(pl.multiple_of(i * 512, 512), 512), :] = jnp.zeros((512, 128), jnp.float32)
        return 0

    lax.fori_loop(0, acc.shape[0] // 512, clear, 0)
    for load in loads:
        load.wait()

    per_row = lanes // UNROLL

    def order(i, _):
        r = i // per_row
        c = i % per_row * UNROLL
        for j in range(UNROLL):
            stage[pos_s[r, c + j], pl.ds(0, channels), :] = kernels_ref[i * UNROLL + j].astype(
                jnp.float32
            )
        return 0

    lax.fori_loop(0, elems // UNROLL, order, 0)

    def multiply(b):
        weight = weights_ref[b].astype(jnp.float32)

        def one(k, _):
            part = stage[pl.ds(k * CHUNK, CHUNK)].reshape(CHUNK * 8, lanes)
            stage[pl.ds(k * CHUNK, CHUNK)] = jnp.dot(
                part, weight, preferred_element_type=jnp.float32
            ).reshape(CHUNK, 8, lanes)
            return 0

        lax.fori_loop(0 if b == 0 else end_s[b - 1, 0], end_s[b, 0], one, 0)

    for b in range(basis_count):
        multiply(b)

    def scatter(i, _):
        r = i // per_row
        c = i % per_row * UNROLL
        for j in range(UNROLL):
            where = pl.ds(row_s[r, c + j], channels, stride=WIDTH)
            acc[where, :] += stage[pos_s[r, c + j], pl.ds(0, channels), :]
        return 0

    lax.fori_loop(0, elems // UNROLL, scatter, 0)

    copies = []
    start = 0
    for k, (out, size) in enumerate(zip(outs, sizes)):
        copies.append(
            pltpu.make_async_copy(acc.at[pl.ds(start, size)], out, copy_sems.at[k])
        )
        start += size
    for copy in copies:
        copy.start()
    for copy in copies:
        copy.wait()


def project(kernels, basis_weights, owner, column, basis, table):
    elems, channels, points = kernels.shape
    counts = PARTS_A + PARTS_A + PARTS_B + PARTS_B
    sizes = [count * channels * WIDTH for count in counts]
    rows = elems // 128
    vmem = pl.BlockSpec(memory_space=pltpu.VMEM)
    outs = pl.pallas_call(
        functools.partial(project_kernel, sizes),
        out_shape=[jax.ShapeDtypeStruct((size, 128), jnp.float32) for size in sizes],
        in_specs=[vmem] * 5 + [pl.BlockSpec(memory_space=pltpu.SMEM)],
        out_specs=[pl.BlockSpec(memory_space=pl.ANY)] * len(sizes),
        scratch_shapes=[
            pltpu.VMEM((rows, 128), jnp.int32),
            pltpu.VMEM((rows, 128), jnp.int32),
            pltpu.VMEM((8, 128), jnp.int32),
            pltpu.SMEM((rows, 128), jnp.int32),
            pltpu.SMEM((rows, 128), jnp.int32),
            pltpu.SMEM((8, 128), jnp.int32),
            pltpu.VMEM((elems + 8 * CHUNK, 8, 128), jnp.float32),
            pltpu.VMEM((128 * 6 * WIDTH, 128), jnp.float32),
            pltpu.SemaphoreType.DMA((3,)),
            pltpu.SemaphoreType.DMA((len(sizes),)),
        ],
        compiler_params=pltpu.CompilerParams(vmem_limit_bytes=48 * 1024 * 1024),
        name="project",
    )(
        kernels,
        basis_weights,
        owner.reshape(rows, 128),
        column.reshape(rows, 128),
        basis.reshape(rows, 128),
        table,
    )
    return [
        out.reshape(count, channels, WIDTH, 128) for out, count in zip(outs, counts)
    ]


def over_core(value):
    return lax.ppermute(value, "lat", CORE)


def over_x(value):
    return lax.ppermute(value, "lat", RING_X)


def over_z(value):
    return lax.ppermute(value, ("lat", "lon"), RING_Z)


def gauss_taps():
    weights = [math.exp(-(offset * offset) / 8.0) for offset in range(-RADIUS, RADIUS + 1)]
    total = 0.0
    for value in weights:
        total = total + value
    return [value / total for value in weights]


def pass_along(padded, axis_pos):
    length = padded.shape[axis_pos] - 2 * RADIUS
    result = None
    for place, factor in enumerate(gauss_taps()):
        term = factor * lax.slice_in_dim(padded, place, place + length, axis=axis_pos)
        result = term if result is None else result + term
    return result


def with_halo(block, axis, dim, width):
    count = lax.axis_size(axis)
    forward = [(i, i + 1) for i in range(count - 1)]
    backward = [(target, source) for source, target in forward]
    low = lax.ppermute(
        lax.slice_in_dim(block, block.shape[dim] - width, None, axis=dim), axis, forward
    )
    high = lax.ppermute(lax.slice_in_dim(block, 0, width, axis=dim), axis, backward)
    return jnp.concatenate([low, block, high], axis=dim)


def local(kernels, basis_weights, owner_block, column_offset, basis_index):
    lat = lax.axis_index("lat")
    lon = lax.axis_index("lon")
    table = lax.dynamic_slice(
        jnp.asarray(block_tables()), (lat, lon, 0, 0), (1, 1, 2, 64)
    ).reshape(2, 64)
    parts = project(
        kernels, basis_weights, owner_block, column_offset, basis_index, table
    )
    keep_a, send_a = parts[0:3], parts[3:6]
    keep_b, send_b = parts[6:11], parts[11:16]

    p2, q4 = keep_a[0] + over_core(send_a[0]), keep_b[0] + over_core(send_b[0])
    x_in, z_in = over_x(p2), over_z(q4)
    p1, q3 = keep_a[1] + over_core(send_a[1]), keep_b[1] + over_core(send_b[1])
    q2 = keep_b[2] + over_core(send_b[2])
    q1 = keep_b[3] + over_core(send_b[3])
    p0 = keep_a[2] + over_core(send_a[2])
    q0 = keep_b[4] + over_core(send_b[4])
    p1 = jnp.concatenate([p1[:3], p1[3:11] + x_in, p1[11:]])
    q3 = jnp.concatenate([q3[:1], q3[1:5] + z_in, q3[5:]])
    x_in = over_x(p1)
    q2 = q2 + over_z(q3)
    q1 = q1 + over_z(q2)
    z_in = over_z(q1)
    a = p0 + x_in[:8] + over_core(x_in[8:])
    b = q0 + z_in[:4] + over_core(z_in[4:])

    v = jnp.stack([a[6] + over_z(a[7]), a[0]])
    v = jnp.stack([a[5], a[1]]) + over_z(v)
    v = jnp.stack([a[4], a[2]]) + over_z(v)
    v = over_z(v)
    final_a = a[3] + v[0] + over_core(v[1])
    w = jnp.stack([b[2] + over_x(b[3]), b[0]])
    w = over_x(w)
    final_b = b[1] + w[0] + over_core(w[1])

    channels = kernels.shape[1]
    final_a = final_a.reshape(channels, GX // 2, GY, 128)
    final_b = final_b.reshape(channels, GX // 2, GY, 128)
    projected = jnp.concatenate([final_a, final_b], axis=1)

    even = lat % 2 == 0
    outward = [
        (2 * x + c, 2 * (x + 2 * c - 1) + 1 - c)
        for x in range(CHIPS)
        for c in range(2)
        if 0 <= x + 2 * c - 1 < CHIPS
    ]
    outer = lax.ppermute(jnp.where(even, final_a, final_b), "lat", outward)
    inner = over_core(jnp.where(even, final_b, final_a))
    along_lat = pass_along(
        jnp.concatenate(
            [jnp.where(even, outer, inner), projected, jnp.where(even, inner, outer)], axis=1
        ),
        1,
    )
    along_lon = pass_along(with_halo(along_lat, "lon", 2, RADIUS), 2)
    smoothed = pass_along(with_halo(along_lon, "dep", 3, RADIUS), 3)
    return (projected, smoothed)


def solution(mesh):
    placed = (
        P(("lat", "lon", "dep"), None, None),
        P(),
        P(("lat", "lon", "dep"), None),
        P(("lat", "lon", "dep")),
        P(("lat", "lon", "dep")),
    )
    return jax.shard_map(
        local,
        mesh=mesh,
        in_specs=placed,
        out_specs=(P(None, "lat", "lon", "dep"), P(None, "lat", "lon", "dep")),
        check_vma=False,
    )
```

time: 447 us -> 167 us (0.37)
  the two profiles are of different devices: /device:TPU:1 before, /device:TPU:100 now
where the time goes in v1:
time: 167 us
  waiting for transfers between devices  59.6 us (36%)
  starting transfers between devices  52.5 us (31%)
  Pallas kernels  42 us (25%)
  local copies, waits for them, and re-layouts  6.61 us (4%)
  other arithmetic  5.11 us (3%)
    pallas_call x1, Pallas kernels, project(): pl.pallas_call(functools.partial(project_kernel, sizes), out_shape=[jax.S...  42 us
    ppermute x8, waiting for transfers between devices, over_z(): return lax.ppermute(value, ('lat', 'lon'), RING_Z)  35 us
    ppermute x8, starting transfers between devices, over_z(): return lax.ppermute(value, ('lat', 'lon'), RING_Z)  29.3 us
    ppermute x2, waiting for transfers between devices, with_halo(): lax.ppermute(lax.slice_in_dim(block, 0, width, axis=dim), axis, backward)  9.63 us
    ppermute x2, starting transfers between devices, with_halo(): lax.ppermute(lax.slice_in_dim(block, block.shape[dim] - width, None, axis...  9.2 us
    ppermute x13, waiting for transfers between devices, over_core(): return lax.ppermute(value, 'lat', CORE)  6.5 us
    ppermute x4, starting transfers between devices, over_x(): return lax.ppermute(value, 'lat', RING_X)  5.77 us
    unnamed x19, local copies, waits for them, and re-layouts  5.56 us
  transfers between devices with their start and end apart: 30, of which 16 were waited for; matrix products, arithmetic and copies ran while one was open for 2% of the time, Pallas kernels for 0%

profile of v1, /device:TPU:100, one launch (start us, length us, event | category | flops | bytes accessed | tf_op | source)
XLA Modules:
  0.0 166.8 jit_solution(11135343584923525121)
XLA Ops:
  0.7 5.5 %copy.8.kernels_ref = bf16[2048,6,128]{2,1,0:T(8,128)(2,1)} copy(bf16[2048,6,128]{2,0,1:T(8,128)(2,1)} %param.6) | data formatting | bytes 6291456 | tf_op args[0]
  6.9 42.0 %project.1 = (f32[1536,128]{1,0:T(8,128)S(1)}, f32[3072,128]{1,0:T(8,128)}, f32[1536,128]{1,0:T(8,128)S(1)}, f32[1536,128]{1,0:T(8,128)S(1)}, f32[3072,128]{1,0:...) custom-call(bf16[2048,6,128]{2,1,0:T(8,128)(2,1)} %copy.8.kernels_re, ...), custom_call_target="tpu_custom_call" | custom-call | tf_op jit(solution)/shard_map/project/pallas_call | solution.py:184
  50.0 5.2 %collective-permute-done.15 = f32[4,6,32,128]{3,2,1,0:T(8,128)S(1)} collective-permute-done((f32[4,6,32,128]{3,2,1,0:T(8,128)S(1)}, f32[4,6,32,128]{3,2,1,0:T(8,128)S(1)}, u32[]{:S(2)}, u32[]{:S(2)}) %collective-permute-start.15) | collective-permute-done | bytes 393248 | tf_op jit(solution)/shard_map/ppermute | solution.py:217
  55.2 2.8 %collective-permute-start.16 = (f32[4,6,32,128]{3,2,1,0:T(8,128)S(1)}, f32[4,6,32,128]{3,2,1,0:T(8,128)S(1)}, u32[]{:S(2)}, u32[]{:S(2)}) collective-permute-start(f32[4,6,32,128]{3,2,1,0:T(8,128)S(1)} %add.178), channel_id=1, source_target_pairs={{0,4},{4,8},{8,12},{12,16},{16,20},{20,24},{24,28},{28,0},{32,60},... | collective-permute-start | bytes 1179656 | tf_op jit(solution)/shard_map/ppermute | solution.py:225
  59.9 3.5 %collective-permute-done.16 = f32[4,6,32,128]{3,2,1,0:T(8,128)S(1)} collective-permute-done((f32[4,6,32,128]{3,2,1,0:T(8,128)S(1)}, f32[4,6,32,128]{3,2,1,0:T(8,128)S(1)}, u32[]{:S(2)}, u32[]{:S(2)}) %collective-permute-start.16) | collective-permute-done | bytes 393248 | tf_op jit(solution)/shard_map/ppermute | solution.py:225
  63.5 3.8 %collective-permute-start.17 = (f32[8,6,32,128]{3,2,1,0:T(8,128)S(1)}, f32[8,6,32,128]{3,2,1,0:T(8,128)S(1)}, u32[]{:S(2)}, u32[]{:S(2)}) collective-permute-start(f32[8,6,32,128]{3,2,1,0:T(8,128)S(1)} %pad_maximum_fusion.1), channel_id=1, source_target_pairs={{0,4},{4,8},{8,12},{12,16},{16,20},{20,24},{24,28},{28,0},{32,60},... | collective-permute-start | bytes 2359304 | tf_op jit(solution)/shard_map/ppermute | solution.py:225
  67.8 2.5 %collective-permute-done.3 = f32[8,6,32,128]{3,2,1,0:T(8,128)S(1)} collective-permute-done((f32[8,6,32,128]{3,2,1,0:T(8,128)S(1)}, f32[8,6,32,128]{3,2,1,0:T(8,128)S(1)}, u32[]{:S(2)}, u32[]{:S(2)}) %collective-permute-start.3) | collective-permute-done | bytes 786464 | tf_op jit(solution)/shard_map/ppermute | solution.py:221
  72.1 4.7 %collective-permute-done.17 = f32[8,6,32,128]{3,2,1,0:T(8,128)S(1)} collective-permute-done((f32[8,6,32,128]{3,2,1,0:T(8,128)S(1)}, f32[8,6,32,128]{3,2,1,0:T(8,128)S(1)}, u32[]{:S(2)}, u32[]{:S(2)}) %collective-permute-start.17) | collective-permute-done | bytes 786464 | tf_op jit(solution)/shard_map/ppermute | solution.py:225
  77.1 3.8 %collective-permute-start.18 = (f32[8,6,32,128]{3,2,1,0:T(8,128)S(1)}, f32[8,6,32,128]{3,2,1,0:T(8,128)S(1)}, u32[]{:S(2)}, u32[]{:S(2)}) collective-permute-start(f32[8,6,32,128]{3,2,1,0:T(8,128)S(1)} %add_add_fusion), channel_id=1, source_target_pairs={{0,4},{4,8},{8,12},{12,16},{16,20},{20,24},{24,28},{28,0},{32,60},... | collective-permute-start | bytes 2359304 | tf_op jit(solution)/shard_map/ppermute | solution.py:225
  80.8 9.5 %collective-permute-done.18 = f32[8,6,32,128]{3,2,1,0:T(8,128)S(1)} collective-permute-done((f32[8,6,32,128]{3,2,1,0:T(8,128)S(1)}, f32[8,6,32,128]{3,2,1,0:T(8,128)S(1)}, u32[]{:S(2)}, u32[]{:S(2)}) %collective-permute-start.18) | collective-permute-done | bytes 786464 | tf_op jit(solution)/shard_map/ppermute | solution.py:225
  90.6 4.0 %collective-permute-start.19 = (f32[8,6,32,128]{3,2,1,0:T(8,128)S(1)}, f32[8,6,32,128]{3,2,1,0:T(8,128)S(1)}, u32[]{:S(2)}, u32[]{:S(2)}) collective-permute-start(f32[8,6,32,128]{3,2,1,0:T(8,128)S(1)} %add_add_fusion.1), channel_id=1, source_target_pairs={{0,4},{4,8},{8,12},{12,16},{16,20},{20,24},{24,28},{28,0},{32,60},... | collective-permute-start | bytes 2359304 | tf_op jit(solution)/shard_map/ppermute | solution.py:225
  95.3 8.8 %collective-permute-done.19 = f32[8,6,32,128]{3,2,1,0:T(8,128)S(1)} collective-permute-done((f32[8,6,32,128]{3,2,1,0:T(8,128)S(1)}, f32[8,6,32,128]{3,2,1,0:T(8,128)S(1)}, u32[]{:S(2)}, u32[]{:S(2)}) %collective-permute-start.19) | collective-permute-done | bytes 786464 | tf_op jit(solution)/shard_map/ppermute | solution.py:225
  104.6 3.8 %collective-permute-start.6 = (f32[6,32,128]{2,1,0:T(8,128)S(1)}, f32[6,32,128]{2,1,0:T(8,128)S(1)}, u32[]{:S(2)}, u32[]{:S(2)}) collective-permute-start(f32[6,32,128]{2,1,0:T(8,128)S(1)} %get-tuple-element.41), channel_id=1, source_target_pairs={{0,4},{4,8},{8,12},{12,16},{16,20},{20,24},{24,28},{28,0},{32,60},... | collective-permute-start | bytes 294920 | tf_op jit(solution)/shard_map/ppermute | solution.py:225
  110.7 3.7 %collective-permute-start.7 = (f32[2,6,32,128]{3,2,1,0:T(8,128)S(1)}, f32[2,6,32,128]{3,2,1,0:T(8,128)S(1)}, u32[]{:S(2)}, u32[]{:S(2)}) collective-permute-start(f32[2,6,32,128]{3,2,1,0:T(8,128)S(1)} %pad_maximum_fusion.8), channel_id=1, source_target_pairs={{0,4},{4,8},{8,12},{12,16},{16,20},{20,24},{24,28},{28,0},{32,60},... | collective-permute-start | bytes 589832 | tf_op jit(solution)/shard_map/ppermute | solution.py:225
  117.6 3.8 %collective-permute-start.8 = (f32[2,6,32,128]{3,2,1,0:T(8,128)S(1)}, f32[2,6,32,128]{3,2,1,0:T(8,128)S(1)}, u32[]{:S(2)}, u32[]{:S(2)}) collective-permute-start(f32[2,6,32,128]{3,2,1,0:T(8,128)S(1)} %maximum_add_fusion.1), channel_id=1, source_target_pairs={{0,4},{4,8},{8,12},{12,16},{16,20},{20,24},{24,28},{28,0},{32,60},... | collective-permute-start | bytes 589832 | tf_op jit(solution)/shard_map/ppermute | solution.py:225
  124.6 3.8 %collective-permute-start.9 = (f32[2,6,32,128]{3,2,1,0:T(8,128)S(1)}, f32[2,6,32,128]{3,2,1,0:T(8,128)S(1)}, u32[]{:S(2)}, u32[]{:S(2)}) collective-permute-start(f32[2,6,32,128]{3,2,1,0:T(8,128)S(1)} %maximum_add_fusion), channel_id=1, source_target_pairs={{0,4},{4,8},{8,12},{12,16},{16,20},{20,24},{24,28},{28,0},{32,60},... | collective-permute-start | bytes 589832 | tf_op jit(solution)/shard_map/ppermute | solution.py:225
  128.4 3.1 %collective-permute-done.9 = f32[2,6,32,128]{3,2,1,0:T(8,128)S(1)} collective-permute-done((f32[2,6,32,128]{3,2,1,0:T(8,128)S(1)}, f32[2,6,32,128]{3,2,1,0:T(8,128)S(1)}, u32[]{:S(2)}, u32[]{:S(2)}) %collective-permute-start.9) | collective-permute-done | bytes 196640 | tf_op jit(solution)/shard_map/ppermute | solution.py:225
  133.1 2.7 %collective-permute-start.24 = (f32[6,4,8,128]{3,2,1,0:T(8,128)S(1)}, f32[6,4,8,128]{3,2,1,0:T(8,128)S(1)}, u32[]{:S(2)}, u32[]{:S(2)}) collective-permute-start(f32[6,4,8,128]{3,2,1,0:T(8,128)S(1)} %get-tuple-element.36), channel_id=1, source_target_pairs={{32,64},{64,32},{96,128},{128,96},{160,192},{192,160},{33,65},{65,... | collective-permute-start | bytes 294920 | tf_op jit(solution)/shard_map/ppermute | solution.py:305
  135.9 3.2 %collective-permute-done.24 = f32[6,4,8,128]{3,2,1,0:T(8,128)S(1)} collective-permute-done((f32[6,4,8,128]{3,2,1,0:T(8,128)S(1)}, f32[6,4,8,128]{3,2,1,0:T(8,128)S(1)}, u32[]{:S(2)}, u32[]{:S(2)}) %collective-permute-start.24) | collective-permute-done | bytes 98336 | tf_op jit(solution)/shard_map/ppermute | solution.py:305
  139.9 5.7 %collective-permute-start.26 = (f32[6,8,4,128]{3,2,1,0:T(4,128)S(1)}, f32[6,8,4,128]{3,2,1,0:T(4,128)S(1)}, u32[]{:S(2)}, u32[]{:S(2)}) collective-permute-start(f32[6,8,4,128]{3,2,1,0:T(4,128)S(1)} %get-tuple-element.49), channel_id=1, source_target_pairs={{0,4},{4,8},{8,12},{12,16},{16,20},{20,24},{24,28},{1,5},{5,9},{9,... | collective-permute-start | bytes 294920 | tf_op jit(solution)/shard_map/ppermute | solution.py:249
  148.2 5.3 %collective-permute-done.27 = f32[6,8,4,128]{3,2,1,0:T(4,128)S(1)} collective-permute-done((f32[6,8,4,128]{3,2,1,0:T(4,128)S(1)}, f32[6,8,4,128]{3,2,1,0:T(4,128)S(1)}, u32[]{:S(2)}, u32[]{:S(2)}) %collective-permute-start.27) | collective-permute-done | bytes 98336 | tf_op jit(solution)/shard_map/ppermute | solution.py:252
  154.0 3.5 %collective-permute-start.28 = (f32[6,8,8,4]{3,2,1,0:T(8,128)S(1)}, f32[6,8,8,4]{3,2,1,0:T(8,128)S(1)}, u32[]{:S(2)}, u32[]{:S(2)}) collective-permute-start(f32[6,8,8,4]{3,2,1,0:T(8,128)S(1)} %get-tuple-element.47), channel_id=1, source_target_pairs={{0,1},{1,2},{2,3},{4,5},{5,6},{6,7},{8,9},{9,10},{10,11},{12,13},{... | collective-permute-start | bytes 18440 | tf_op jit(solution)/shard_map/ppermute | solution.py:249
  158.8 2.2 %collective-permute-done.28 = f32[6,8,8,4]{3,2,1,0:T(8,128)S(1)} collective-permute-done((f32[6,8,8,4]{3,2,1,0:T(8,128)S(1)}, f32[6,8,8,4]{3,2,1,0:T(8,128)S(1)}, u32[]{:S(2)}, u32[]{:S(2)}) %collective-permute-start.28) | collective-permute-done | bytes 6176 | tf_op jit(solution)/shard_map/ppermute | solution.py:249
  161.0 4.3 %collective-permute-done.29 = f32[6,8,8,4]{3,2,1,0:T(8,128)S(1)} collective-permute-done((f32[6,8,8,4]{3,2,1,0:T(8,128)S(1)}, f32[6,8,8,4]{3,2,1,0:T(8,128)S(1)}, u32[]{:S(2)}, u32[]{:S(2)}) %collective-permute-start.29) | collective-permute-done | bytes 6176 | tf_op jit(solution)/shard_map/ppermute | solution.py:252
  (94 shorter events, 24.8 us)
Async XLA Ops:
  48.9 18.4 %collective-permute-start.1 = (f32[16,6,32,128]{3,2,1,0:T(8,128)}, f32[16,6,32,128]{3,2,1,0:T(8,128)S(1)}, u32[]{:S(2)}, u32[]{:S(2)}) collective-permute-start(f32[16,6,32,128]{3,2,1,0:T(8,128)} %bitcast.80), channel_id=1, source_target_pairs={{0,32},{32,0},{64,96},{96,64},{128,160},{160,128},{192,224},{224,1... | collective-permute-start | bytes 4718600 | tf_op jit(solution)/shard_map/ppermute | solution.py:217
  49.1 9.0 %collective-permute-start.2 = (f32[8,6,32,128]{3,2,1,0:T(8,128)S(1)}, f32[8,6,32,128]{3,2,1,0:T(8,128)S(1)}, u32[]{:S(2)}, u32[]{:S(2)}) collective-permute-start(f32[8,6,32,128]{3,2,1,0:T(8,128)S(1)} %bitcast.74), channel_id=1, source_target_pairs={{0,32},{32,0},{64,96},{96,64},{128,160},{160,128},{192,224},{224,1... | collective-permute-start | bytes 2359304 | tf_op jit(solution)/shard_map/ppermute | solution.py:217
  49.5 10.2 %collective-permute-start.14 = (f32[8,6,32,128]{3,2,1,0:T(8,128)}, f32[8,6,32,128]{3,2,1,0:T(8,128)S(1)}, u32[]{:S(2)}, u32[]{:S(2)}) collective-permute-start(f32[8,6,32,128]{3,2,1,0:T(8,128)} %bitcast.83), channel_id=1, source_target_pairs={{0,32},{32,0},{64,96},{96,64},{128,160},{160,128},{192,224},{224,1... | collective-permute-start | bytes 2359304 | tf_op jit(solution)/shard_map/ppermute | solution.py:217
  55.2 8.1 %collective-permute-start.16 = (f32[4,6,32,128]{3,2,1,0:T(8,128)S(1)}, f32[4,6,32,128]{3,2,1,0:T(8,128)S(1)}, u32[]{:S(2)}, u32[]{:S(2)}) collective-permute-start(f32[4,6,32,128]{3,2,1,0:T(8,128)S(1)} %add.178), channel_id=1, source_target_pairs={{0,4},{4,8},{8,12},{12,16},{16,20},{20,24},{24,28},{28,0},{32,60},... | collective-permute-start | bytes 1179656 | tf_op jit(solution)/shard_map/ppermute | solution.py:225
  58.2 12.1 %collective-permute-start.3 = (f32[8,6,32,128]{3,2,1,0:T(8,128)S(1)}, f32[8,6,32,128]{3,2,1,0:T(8,128)S(1)}, u32[]{:S(2)}, u32[]{:S(2)}) collective-permute-start(f32[8,6,32,128]{3,2,1,0:T(8,128)S(1)} %add.164), channel_id=1, source_target_pairs={{0,64},{32,224},{64,128},{96,32},{128,192},{160,96},{192,0},{224,1... | collective-permute-start | bytes 2359304 | tf_op jit(solution)/shard_map/ppermute | solution.py:221
  59.7 12.5 %collective-permute-start.13 = (f32[8,6,32,128]{3,2,1,0:T(8,128)S(1)}, f32[8,6,32,128]{3,2,1,0:T(8,128)S(1)}, u32[]{:S(2)}, u32[]{:S(2)}) collective-permute-start(f32[8,6,32,128]{3,2,1,0:T(8,128)S(1)} %bitcast.82), channel_id=1, source_target_pairs={{0,32},{32,0},{64,96},{96,64},{128,160},{160,128},{192,224},{224,1... | collective-permute-start | bytes 2359304 | tf_op jit(solution)/shard_map/ppermute | solution.py:217
  63.5 13.3 %collective-permute-start.17 = (f32[8,6,32,128]{3,2,1,0:T(8,128)S(1)}, f32[8,6,32,128]{3,2,1,0:T(8,128)S(1)}, u32[]{:S(2)}, u32[]{:S(2)}) collective-permute-start(f32[8,6,32,128]{3,2,1,0:T(8,128)S(1)} %pad_maximum_fusion.1), channel_id=1, source_target_pairs={{0,4},{4,8},{8,12},{12,16},{16,20},{20,24},{24,28},{28,0},{32,60},... | collective-permute-start | bytes 2359304 | tf_op jit(solution)/shard_map/ppermute | solution.py:225
  70.7 23.9 %collective-permute-start.4 = (f32[16,6,32,128]{3,2,1,0:T(8,128)S(1)}, f32[16,6,32,128]{3,2,1,0:T(8,128)S(1)}, u32[]{:S(2)}, u32[]{:S(2)}) collective-permute-start(f32[16,6,32,128]{3,2,1,0:T(8,128)S(1)} %pad_maximum_fusion), channel_id=1, source_target_pairs={{0,64},{32,224},{64,128},{96,32},{128,192},{160,96},{192,0},{224,1... | collective-permute-start | bytes 4718600 | tf_op jit(solution)/shard_map/ppermute | solution.py:221
  72.1 8.7 %collective-permute-start.12 = (f32[8,6,32,128]{3,2,1,0:T(8,128)S(1)}, f32[8,6,32,128]{3,2,1,0:T(8,128)S(1)}, u32[]{:S(2)}, u32[]{:S(2)}) collective-permute-start(f32[8,6,32,128]{3,2,1,0:T(8,128)S(1)} %bitcast.81), channel_id=1, source_target_pairs={{0,32},{32,0},{64,96},{96,64},{128,160},{160,128},{192,224},{224,1... | collective-permute-start | bytes 2359304 | tf_op jit(solution)/shard_map/ppermute | solution.py:217
  77.1 13.3 %collective-permute-start.18 = (f32[8,6,32,128]{3,2,1,0:T(8,128)S(1)}, f32[8,6,32,128]{3,2,1,0:T(8,128)S(1)}, u32[]{:S(2)}, u32[]{:S(2)}) collective-permute-start(f32[8,6,32,128]{3,2,1,0:T(8,128)S(1)} %add_add_fusion), channel_id=1, source_target_pairs={{0,4},{4,8},{8,12},{12,16},{16,20},{20,24},{24,28},{28,0},{32,60},... | collective-permute-start | bytes 2359304 | tf_op jit(solution)/shard_map/ppermute | solution.py:225
  90.6 13.5 %collective-permute-start.19 = (f32[8,6,32,128]{3,2,1,0:T(8,128)S(1)}, f32[8,6,32,128]{3,2,1,0:T(8,128)S(1)}, u32[]{:S(2)}, u32[]{:S(2)}) collective-permute-start(f32[8,6,32,128]{3,2,1,0:T(8,128)S(1)} %add_add_fusion.1), channel_id=1, source_target_pairs={{0,4},{4,8},{8,12},{12,16},{16,20},{20,24},{24,28},{28,0},{32,60},... | collective-permute-start | bytes 2359304 | tf_op jit(solution)/shard_map/ppermute | solution.py:225
  94.6 9.6 %collective-permute-start = (f32[8,6,32,128]{3,2,1,0:T(8,128)S(1)}, f32[8,6,32,128]{3,2,1,0:T(8,128)S(1)}, u32[]{:S(2)}, u32[]{:S(2)}) collective-permute-start(f32[8,6,32,128]{3,2,1,0:T(8,128)S(1)} %bitcast.73), channel_id=1, source_target_pairs={{0,32},{32,0},{64,96},{96,64},{128,160},{160,128},{192,224},{224,1... | collective-permute-start | bytes 2359304 | tf_op jit(solution)/shard_map/ppermute | solution.py:217
  94.6 9.6 %collective-permute-start.5 = (f32[8,6,32,128]{3,2,1,0:T(8,128)S(1)}, f32[8,6,32,128]{3,2,1,0:T(8,128)S(1)}, u32[]{:S(2)}, u32[]{:S(2)}) collective-permute-start(f32[8,6,32,128]{3,2,1,0:T(8,128)S(1)} %slice.238), channel_id=1, source_target_pairs={{0,32},{32,0},{64,96},{96,64},{128,160},{160,128},{192,224},{224,1... | collective-permute-start | bytes 2359304 | tf_op jit(solution)/shard_map/ppermute | solution.py:217
  95.2 13.2 %collective-permute-start.11 = (f32[4,6,32,128]{3,2,1,0:T(8,128)S(1)}, f32[4,6,32,128]{3,2,1,0:T(8,128)S(1)}, u32[]{:S(2)}, u32[]{:S(2)}) collective-permute-start(f32[4,6,32,128]{3,2,1,0:T(8,128)S(1)} %bitcast.75), channel_id=1, source_target_pairs={{0,32},{32,0},{64,96},{96,64},{128,160},{160,128},{192,224},{224,1... | collective-permute-start | bytes 1179656 | tf_op jit(solution)/shard_map/ppermute | solution.py:217
  104.6 6.0 %collective-permute-start.6 = (f32[6,32,128]{2,1,0:T(8,128)S(1)}, f32[6,32,128]{2,1,0:T(8,128)S(1)}, u32[]{:S(2)}, u32[]{:S(2)}) collective-permute-start(f32[6,32,128]{2,1,0:T(8,128)S(1)} %get-tuple-element.41), channel_id=1, source_target_pairs={{0,4},{4,8},{8,12},{12,16},{16,20},{20,24},{24,28},{28,0},{32,60},... | collective-permute-start | bytes 294920 | tf_op jit(solution)/shard_map/ppermute | solution.py:225
  110.7 6.9 %collective-permute-start.7 = (f32[2,6,32,128]{3,2,1,0:T(8,128)S(1)}, f32[2,6,32,128]{3,2,1,0:T(8,128)S(1)}, u32[]{:S(2)}, u32[]{:S(2)}) collective-permute-start(f32[2,6,32,128]{3,2,1,0:T(8,128)S(1)} %pad_maximum_fusion.8), channel_id=1, source_target_pairs={{0,4},{4,8},{8,12},{12,16},{16,20},{20,24},{24,28},{28,0},{32,60},... | collective-permute-start | bytes 589832 | tf_op jit(solution)/shard_map/ppermute | solution.py:225
  114.4 7.0 %collective-permute-start.21 = (f32[6,32,128]{2,1,0:T(8,128)S(1)}, f32[6,32,128]{2,1,0:T(8,128)S(1)}, u32[]{:S(2)}, u32[]{:S(2)}) collective-permute-start(f32[6,32,128]{2,1,0:T(8,128)S(1)} %get-tuple-element.45), channel_id=1, source_target_pairs={{0,64},{32,224},{64,128},{96,32},{128,192},{160,96},{192,0},{224,1... | collective-permute-start | bytes 294920 | tf_op jit(solution)/shard_map/ppermute | solution.py:221
  117.6 7.0 %collective-permute-start.8 = (f32[2,6,32,128]{3,2,1,0:T(8,128)S(1)}, f32[2,6,32,128]{3,2,1,0:T(8,128)S(1)}, u32[]{:S(2)}, u32[]{:S(2)}) collective-permute-start(f32[2,6,32,128]{3,2,1,0:T(8,128)S(1)} %maximum_add_fusion.1), channel_id=1, source_target_pairs={{0,4},{4,8},{8,12},{12,16},{16,20},{20,24},{24,28},{28,0},{32,60},... | collective-permute-start | bytes 589832 | tf_op jit(solution)/shard_map/ppermute | solution.py:225
  121.4 6.9 %collective-permute-start.22 = (f32[2,6,32,128]{3,2,1,0:T(8,128)S(1)}, f32[2,6,32,128]{3,2,1,0:T(8,128)S(1)}, u32[]{:S(2)}, u32[]{:S(2)}) collective-permute-start(f32[2,6,32,128]{3,2,1,0:T(8,128)S(1)} %pad_maximum_fusion.9), channel_id=1, source_target_pairs={{0,64},{32,224},{64,128},{96,32},{128,192},{160,96},{192,0},{224,1... | collective-permute-start | bytes 589832 | tf_op jit(solution)/shard_map/ppermute | solution.py:221
  124.6 7.0 %collective-permute-start.9 = (f32[2,6,32,128]{3,2,1,0:T(8,128)S(1)}, f32[2,6,32,128]{3,2,1,0:T(8,128)S(1)}, u32[]{:S(2)}, u32[]{:S(2)}) collective-permute-start(f32[2,6,32,128]{3,2,1,0:T(8,128)S(1)} %maximum_add_fusion), channel_id=1, source_target_pairs={{0,4},{4,8},{8,12},{12,16},{16,20},{20,24},{24,28},{28,0},{32,60},... | collective-permute-start | bytes 589832 | tf_op jit(solution)/shard_map/ppermute | solution.py:225
  139.9 8.3 %collective-permute-start.26 = (f32[6,8,4,128]{3,2,1,0:T(4,128)S(1)}, f32[6,8,4,128]{3,2,1,0:T(4,128)S(1)}, u32[]{:S(2)}, u32[]{:S(2)}) collective-permute-start(f32[6,8,4,128]{3,2,1,0:T(4,128)S(1)} %get-tuple-element.49), channel_id=1, source_target_pairs={{0,4},{4,8},{8,12},{12,16},{16,20},{20,24},{24,28},{1,5},{5,9},{9,... | collective-permute-start | bytes 294920 | tf_op jit(solution)/shard_map/ppermute | solution.py:249
  145.7 7.9 %collective-permute-start.27 = (f32[6,8,4,128]{3,2,1,0:T(4,128)S(1)}, f32[6,8,4,128]{3,2,1,0:T(4,128)S(1)}, u32[]{:S(2)}, u32[]{:S(2)}) collective-permute-start(f32[6,8,4,128]{3,2,1,0:T(4,128)S(1)} %get-tuple-element.50), channel_id=1, source_target_pairs={{4,0},{8,4},{12,8},{16,12},{20,16},{24,20},{28,24},{5,1},{9,5},{13... | collective-permute-start | bytes 294920 | tf_op jit(solution)/shard_map/ppermute | solution.py:252
  154.0 7.0 %collective-permute-start.28 = (f32[6,8,8,4]{3,2,1,0:T(8,128)S(1)}, f32[6,8,8,4]{3,2,1,0:T(8,128)S(1)}, u32[]{:S(2)}, u32[]{:S(2)}) collective-permute-start(f32[6,8,8,4]{3,2,1,0:T(8,128)S(1)} %get-tuple-element.47), channel_id=1, source_target_pairs={{0,1},{1,2},{2,3},{4,5},{5,6},{6,7},{8,9},{9,10},{10,11},{12,13},{... | collective-permute-start | bytes 18440 | tf_op jit(solution)/shard_map/ppermute | solution.py:249
  157.5 7.8 %collective-permute-start.29 = (f32[6,8,8,4]{3,2,1,0:T(8,128)S(1)}, f32[6,8,8,4]{3,2,1,0:T(8,128)S(1)}, u32[]{:S(2)}, u32[]{:S(2)}) collective-permute-start(f32[6,8,8,4]{3,2,1,0:T(8,128)S(1)} %get-tuple-element.48), channel_id=1, source_target_pairs={{1,0},{2,1},{3,2},{5,4},{6,5},{7,6},{9,8},{10,9},{11,10},{13,12},{... | collective-permute-start | bytes 18440 | tf_op jit(solution)/shard_map/ppermute | solution.py:252
  (15 other events, 81.6 us)

commit v2 on v1

v2 whole, which is shorter than its diff:
```python
import math

import jax
import jax.numpy as jnp
import numpy as np
from jax import lax
from jax.experimental import pallas as pl
from jax.experimental.pallas import tpu as pltpu
from jax.sharding import PartitionSpec as P

GX = 8
GY = 8
RADIUS = 4
CHIPS = 4
LON = 8
CHUNK = 128
COLS = (5, 3)
GROUP = 4

CORE = [(i, i ^ 1) for i in range(2 * CHIPS)]
RING_X = [(2 * x + c, 2 * ((x + 1 - 2 * c) % CHIPS) + c) for x in range(CHIPS) for c in range(2)]
RING_Z = [
    (lat * LON + z, lat * LON + (z + 1 - 2 * (lat % 2)) % LON)
    for lat in range(2 * CHIPS)
    for z in range(LON)
]

A_P2 = [[(3, 1), (4, 1), (5, 1)], [(0, 1), (1, 1), (2, 1), (6, 1), (7, 1)]]
A_MINE = [[(3, 0), (3, 1), (4, 1)], [(2, 0), (1, 0), (0, 1), (1, 1), (2, 1)]]
A_THEIRS = [[(5, 1), (5, 0), (4, 0)], [(6, 1), (7, 1), (0, 0), (7, 0), (6, 0)]]
LAYOUT_A = (
    [(2, q, own) for part in A_P2 for q, own in part]
    + [(1, q, own) for mine, theirs in zip(A_MINE, A_THEIRS) for q, own in mine + theirs]
    + [(0, q, own) for mine in A_MINE for q, own in mine]
)
B_MINE = [(1, 0), (0, 1), (1, 1), (2, 1)]
B_THEIRS = [(3, 1), (0, 0), (3, 0), (2, 0)]
LAYOUT_B = (
    [(p, 4, 1) for p in range(CHIPS)]
    + [(p, q, own) for q in (3, 2, 1) for p, own in B_MINE + B_THEIRS]
    + [(p, 0, own) for p, own in B_MINE]
)
PARTS_A = (3, 5, 6, 10, 3, 5)
PARTS_B = (4, 8, 8, 8, 4)


def block_tables():
    table = np.zeros((2 * CHIPS, LON, 2, 2 * CHIPS * LON), np.int32)
    for lat in range(2 * CHIPS):
        for z in range(LON):
            for owner in range(2 * CHIPS * LON):
                core = owner // LON % 2
                dx = (owner // LON // 2 - lat // 2) % CHIPS
                dz = (owner % LON - z) % LON
                by_x = {0: None, 1: 0, 2: core, 3: 1}[dx]
                by_z = {0: None, 4: core}.get(dz, 0 if dz < 4 else 1)
                for half, (first, second, layout) in enumerate(
                    ((by_x, by_z, LAYOUT_A), (by_z, by_x, LAYOUT_B))
                ):
                    handler = first if first is not None else second if second is not None else core
                    sign = 1 - 2 * handler
                    place = layout.index((dx * sign % CHIPS, dz * sign % LON, int(core == handler)))
                    block = (0 if handler == lat % 2 else 32) + place
                    table[lat, z, half, owner] = GY * (
                        64 * COLS[0] * half + block * COLS[half]
                    )
    return table


def project_kernel(
    kernels_ref,
    weights_ref,
    owner_ref,
    column_ref,
    basis_ref,
    table_ref,
    acc,
    raw,
    plain,
    stage,
    pos_v,
    row_v,
    end_v,
    pos_s,
    row_s,
    end_s,
    raw_sems,
    sems,
):
    rows, lanes = owner_ref.shape
    basis_count = weights_ref.shape[0]
    channels, elems, _ = kernels_ref.shape
    pitch = plain.shape[0] // channels

    fetches = [
        pltpu.make_async_copy(kernels_ref.at[c], raw.at[c], raw_sems.at[c])
        for c in range(channels)
    ]
    for fetch in fetches:
        fetch.start()

    owner = owner_ref[...]
    column = column_ref[...]
    first = jnp.zeros((rows, lanes), jnp.int32)
    second = jnp.zeros((rows, lanes), jnp.int32)
    for o in range(table_ref.shape[1]):
        hit = owner == o
        first = jnp.where(hit, table_ref[0, o], first)
        second = jnp.where(hit, table_ref[1, o], second)
    width = GY * COLS[0]
    row = jnp.where(column < width, first + column, second + column - width)
    row_v[...] = row * channels

    basis = basis_ref[...]
    upper = (
        lax.broadcasted_iota(jnp.int32, (lanes, lanes), 0)
        <= lax.broadcasted_iota(jnp.int32, (lanes, lanes), 1)
    ).astype(jnp.float32)
    lower = (
        lax.broadcasted_iota(jnp.int32, (rows, rows), 1)
        < lax.broadcasted_iota(jnp.int32, (rows, rows), 0)
    ).astype(jnp.float32)
    base = jnp.zeros((1, lanes), jnp.int32)
    pos = jnp.zeros((rows, lanes), jnp.int32)
    for b in range(basis_count):
        hit = basis == b
        inside = jnp.dot(hit.astype(jnp.float32), upper, preferred_element_type=jnp.float32)
        in_row = jnp.broadcast_to(inside[:, lanes - 1 :], (rows, lanes))
        before = jnp.dot(lower, in_row, preferred_element_type=jnp.float32)
        rank = (before + inside).astype(jnp.int32) - 1
        total = (before + in_row)[rows - 1 :].astype(jnp.int32)
        pos = jnp.where(hit, base + rank, pos)
        base = base + (total + CHUNK - 1) // CHUNK * CHUNK
        end_v[pl.ds(b, 1), :] = base // CHUNK
    pos_v[...] = pos * channels
    loads = [
        pltpu.make_async_copy(source, target, sems.at[i])
        for i, (source, target) in enumerate(
            ((pos_v, pos_s), (row_v, row_s), (end_v, end_s))
        )
    ]
    for load in loads:
        load.start()

    def clear(i, _):
        acc[pl.ds(pl.multiple_of(i * 512, 512), 512), :] = jnp.zeros((512, 128), jnp.float32)
        return 0

    lax.fori_loop(0, acc.shape[0] // 512, clear, 0)

    for c, fetch in enumerate(fetches):
        fetch.wait()

        def widen(i, _):
            start = pl.multiple_of(i * 256, 256)
            plain[pl.ds(c * pitch + start, 256), :] = raw[c, pl.ds(start, 256), :].astype(
                jnp.float32
            )
            return 0

        lax.fori_loop(0, elems // 256, widen, 0)
    for load in loads:
        load.wait()

    def order(r, _):
        for j in range(lanes):
            stage[pl.ds(pos_s[r, j], channels), :] = plain[
                pl.ds(r * lanes + j, channels, stride=pitch), :
            ]
        return 0

    lax.fori_loop(0, rows, order, 0)

    def multiply(b):
        weight = weights_ref[b]

        def one(k, _):
            where = pl.ds(pl.multiple_of(k * (CHUNK * channels), CHUNK * channels), CHUNK * channels)
            stage[where, :] = jnp.dot(
                stage[where, :].astype(jnp.bfloat16), weight, preferred_element_type=jnp.float32
            )
            return 0

        lax.fori_loop(0 if b == 0 else end_s[b - 1, 0], end_s[b, 0], one, 0)

    for b in range(basis_count):
        multiply(b)

    def scatter(r, _):
        for j in range(0, lanes, GROUP):
            targets = [row_s[r, j + i] for i in range(GROUP)]
            sums = [acc[pl.ds(target, channels), :] for target in targets]
            terms = [stage[pl.ds(pos_s[r, j + i], channels), :] for i in range(GROUP)]
            for i in range(GROUP):
                sums[i] = sums[i] + terms[i]
                for h in range(i):
                    sums[i] = sums[i] + jnp.where(targets[i] == targets[h], terms[h], 0.0)
            for target, value in zip(targets, sums):
                acc[pl.ds(target, channels), :] = value
        return 0

    lax.fori_loop(0, rows, scatter, 0)


def project(kernels, basis_weights, owner, column, basis, table):
    elems, channels, points = kernels.shape
    rows = elems // 128
    room = elems + 8 * CHUNK
    pitch = elems + 8
    vmem = pl.BlockSpec(memory_space=pltpu.VMEM)
    total = 64 * GX * GY * channels
    acc = pl.pallas_call(
        project_kernel,
        out_shape=pltpu.VMEM((total, 128), jnp.float32),
        in_specs=[pl.BlockSpec(memory_space=pl.ANY)]
        + [vmem] * 4
        + [pl.BlockSpec(memory_space=pltpu.SMEM)],
        out_specs=vmem,
        scratch_shapes=[
            pltpu.VMEM((channels, elems, 128), jnp.bfloat16),
            pltpu.VMEM((channels * pitch, 128), jnp.float32),
            pltpu.VMEM((channels * room, 128), jnp.float32),
            pltpu.VMEM((rows, 128), jnp.int32),
            pltpu.VMEM((rows, 128), jnp.int32),
            pltpu.VMEM((8, 128), jnp.int32),
            pltpu.SMEM((rows, 128), jnp.int32),
            pltpu.SMEM((rows, 128), jnp.int32),
            pltpu.SMEM((8, 128), jnp.int32),
            pltpu.SemaphoreType.DMA((channels,)),
            pltpu.SemaphoreType.DMA((3,)),
        ],
        compiler_params=pltpu.CompilerParams(vmem_limit_bytes=48 * 1024 * 1024),
        name="project",
    )(
        jnp.transpose(kernels, (1, 0, 2)),
        basis_weights,
        owner.reshape(rows, 128),
        column.reshape(rows, 128),
        basis.reshape(rows, 128),
        table,
    )
    parts = []
    start = 0
    for counts, cols in ((PARTS_A * 2, COLS[0]), (PARTS_B * 2, COLS[1])):
        size = cols * GY * channels
        for count in counts:
            parts.append(acc[start : start + count * size].reshape(count, size, 128))
            start += count * size
    return parts


def over_core(value):
    return lax.ppermute(value, "lat", CORE)


def over_x(value):
    return lax.ppermute(value, "lat", RING_X)


def over_z(value):
    return lax.ppermute(value, ("lat", "lon"), RING_Z)


def add_at(block, part, start):
    end = start + part.shape[0]
    return jnp.concatenate([block[:start], block[start:end] + part, block[end:]])


def gauss_taps():
    weights = [math.exp(-(offset * offset) / 8.0) for offset in range(-RADIUS, RADIUS + 1)]
    total = 0.0
    for value in weights:
        total = total + value
    return [value / total for value in weights]


def pass_along(padded, axis_pos):
    length = padded.shape[axis_pos] - 2 * RADIUS
    result = None
    for place, factor in enumerate(gauss_taps()):
        term = factor * lax.slice_in_dim(padded, place, place + length, axis=axis_pos)
        result = term if result is None else result + term
    return result


def with_halo(block, axis, dim, width):
    count = lax.axis_size(axis)
    forward = [(i, i + 1) for i in range(count - 1)]
    backward = [(target, source) for source, target in forward]
    low = lax.ppermute(
        lax.slice_in_dim(block, block.shape[dim] - width, None, axis=dim), axis, forward
    )
    high = lax.ppermute(lax.slice_in_dim(block, 0, width, axis=dim), axis, backward)
    return jnp.concatenate([low, block, high], axis=dim)


def local(kernels, basis_weights, owner_block, column_offset, basis_index):
    lat = lax.axis_index("lat")
    lon = lax.axis_index("lon")
    table = lax.dynamic_slice(
        jnp.asarray(block_tables()), (lat, lon, 0, 0), (1, 1, 2, 64)
    ).reshape(2, 64)
    parts = project(
        kernels, basis_weights, owner_block, column_offset, basis_index, table
    )
    keep_a, send_a = parts[0:6], parts[6:12]
    keep_b, send_b = parts[12:17], parts[17:22]

    p2 = [keep_a[0] + over_core(send_a[0]), None]
    q4 = keep_b[0] + over_core(send_b[0])
    z_in = over_z(q4)
    x_in = [over_x(p2[0]), None]
    p2[1] = keep_a[1] + over_core(send_a[1])
    x_in[1] = over_x(p2[1])
    p1 = [keep_a[2 + i] + over_core(send_a[2 + i]) for i in range(2)]
    q3 = keep_b[1] + over_core(send_b[1])
    q2 = keep_b[2] + over_core(send_b[2])
    q1 = keep_b[3] + over_core(send_b[3])
    p0 = [keep_a[4 + i] + over_core(send_a[4 + i]) for i in range(2)]
    q0 = keep_b[4] + over_core(send_b[4])

    x_in[0] = over_x(add_at(p1[0], x_in[0], 1))
    z_in = over_z(add_at(q3, z_in, 1))
    x_in[1] = over_x(add_at(p1[1], x_in[1], 2))
    z_in = over_z(q2 + z_in)
    near = p0[0] + x_in[0][:3] + over_core(x_in[0][3:])
    v = over_z(near[2:])
    z_in = over_z(q1 + z_in)
    v = over_z(jnp.concatenate([near[1:2] + v, near[:1]]))
    far = p0[1] + x_in[1][:5] + over_core(x_in[1][5:])
    v = over_z(jnp.concatenate([far[4:] + v[:1], far[:1] + v[1:]]))
    b = q0 + z_in[:4] + over_core(z_in[4:])
    w = over_x(b[3:])
    v = over_z(jnp.concatenate([far[3:4] + v[:1], far[1:2] + v[1:]]))
    w = over_x(jnp.concatenate([b[2:3] + w, b[:1]]))
    final_a = far[2] + v[0] + over_core(v[1])
    final_b = b[1] + w[0] + over_core(w[1])

    channels = kernels.shape[1]
    final_a = jnp.transpose(final_a.reshape(COLS[0], GY, channels, 128), (2, 0, 1, 3))
    final_b = jnp.transpose(final_b.reshape(COLS[1], GY, channels, 128), (2, 0, 1, 3))
    projected = jnp.concatenate([final_a, final_b], axis=1)

    even = lat % 2 == 0
    outward = [
        (2 * x + c, 2 * (x + 2 * c - 1) + 1 - c)
        for x in range(CHIPS)
        for c in range(2)
        if 0 <= x + 2 * c - 1 < CHIPS
    ]
    low, high = projected[:, :RADIUS], projected[:, GX - RADIUS :]
    outer = lax.ppermute(jnp.where(even, low, high), "lat", outward)
    inner = over_core(jnp.where(even, high, low))
    along_lat = pass_along(
        jnp.concatenate(
            [jnp.where(even, outer, inner), projected, jnp.where(even, inner, outer)], axis=1
        ),
        1,
    )
    along_lon = pass_along(with_halo(along_lat, "lon", 2, RADIUS), 2)
    smoothed = pass_along(with_halo(along_lon, "dep", 3, RADIUS), 3)
    return (projected, smoothed)


def solution(mesh):
    placed = (
        P(("lat", "lon", "dep"), None, None),
        P(),
        P(("lat", "lon", "dep"), None),
        P(("lat", "lon", "dep")),
        P(("lat", "lon", "dep")),
    )
    return jax.shard_map(
        local,
        mesh=mesh,
        in_specs=placed,
        out_specs=(P(None, "lat", "lon", "dep"), P(None, "lat", "lon", "dep")),
        check_vma=False,
    )
```

time: 167 us -> 126 us (0.75)
  the two profiles are of different devices: /device:TPU:100 before, /device:TPU:1 now
where the time goes in v2:
time: 126 us; the launch traced here: 125 us
  starting transfers between devices  64.7 us (51%)
  waiting for transfers between devices  35.5 us (28%)
  Pallas kernels  16.2 us (13%)
  local copies, waits for them, and re-layouts  3.88 us (3%)
  other arithmetic  3.29 us (3%)
    ppermute x17, starting transfers between devices, over_core(): return lax.ppermute(value, 'lat', CORE)  21.7 us
    ppermute x8, starting transfers between devices, over_z(): return lax.ppermute(value, ('lat', 'lon'), RING_Z)  21.7 us
    ppermute x8, waiting for transfers between devices, over_z(): return lax.ppermute(value, ('lat', 'lon'), RING_Z)  19.2 us
    pallas_call x1, Pallas kernels, project(): pl.pallas_call(project_kernel, out_shape=pltpu.VMEM((total, 128), jnp.flo...  16.2 us
    ppermute x6, starting transfers between devices, over_x(): return lax.ppermute(value, 'lat', RING_X)  8.79 us
    ppermute x2, starting transfers between devices, with_halo(): lax.ppermute(lax.slice_in_dim(block, block.shape[dim] - width, None, axis...  8 us
    ppermute x6, waiting for transfers between devices, over_x(): return lax.ppermute(value, 'lat', RING_X)  4.78 us
    ppermute x1, waiting for transfers between devices, local(): outer = lax.ppermute(jnp.where(even, low, high), 'lat', outward)  4.35 us
  transfers between devices with their start and end apart: 36, of which 16 were waited for; matrix products, arithmetic and copies ran while one was open for 3% of the time, Pallas kernels for 0%

profile of v2, /device:TPU:1, one launch (start us, length us, event | category | flops | bytes accessed | tf_op | source)
XLA Modules:
  0.0 124.6 jit_solution(5173317672797266259)
XLA Ops:
  1.9 16.2 %project.1 = f32[24576,128]{1,0:T(8,128)S(1)} custom-call(bf16[6,2048,128]{2,1,0:T(8,128)(2,1)} %bitcast.46, bf16[8,128,128]{2,1,0:T(8,128)(2,1)} %weights_ref.1, s32[16,128]{1,0:T(8,128)} %bitcast.71, s32[16,128]{1,0:T(8,128)} %bitcast.72, s32[16,128]{1,0:T(8,128)} %bitcast.73, s32[2,64]{1,0:T(2,128)} %dynamic-slice_bitcast_fusion.table_ref), custom_call_target="tpu_custom_call" | custom-call | tf_op jit(solution)/shard_map/project/pallas_call | solution.py:212
  18.2 3.1 %collective-permute-start.7 = (f32[6,240,128]{2,1,0:T(8,128)S(1)}, f32[6,240,128]{2,1,0:T(8,128)S(1)}, u32[]{:S(2)}, u32[]{:S(2)}) collective-permute-start(f32[6,240,128]{2,1,0:T(8,128)S(1)} %bitcast.61), channel_id=1, source_target_pairs={{0,32},{32,0},{64,96},{96,64},{128,160},{160,128},{192,224},{224,1... | collective-permute-start | bytes 2211848 | tf_op jit(solution)/shard_map/ppermute | solution.py:253
  25.0 4.1 %collective-permute-start.22 = (f32[4,144,128]{2,1,0:T(8,128)S(1)}, f32[4,144,128]{2,1,0:T(8,128)S(1)}, u32[]{:S(2)}, u32[]{:S(2)}) collective-permute-start(f32[4,144,128]{2,1,0:T(8,128)S(1)} %add.210), channel_id=1, source_target_pairs={{0,4},{4,8},{8,12},{12,16},{16,20},{20,24},{24,28},{28,0},{32,60},... | collective-permute-start | bytes 884744 | tf_op jit(solution)/shard_map/ppermute | solution.py:261
  30.1 2.7 %collective-permute-done.22 = f32[4,144,128]{2,1,0:T(8,128)S(1)} collective-permute-done((f32[4,144,128]{2,1,0:T(8,128)S(1)}, f32[4,144,128]{2,1,0:T(8,128)S(1)}, u32[]{:S(2)}, u32[]{:S(2)}) %collective-permute-start.22) | collective-permute-done | bytes 294944 | tf_op jit(solution)/shard_map/ppermute | solution.py:261
  32.8 2.1 %collective-permute-start.9 = (f32[3,240,128]{2,1,0:T(8,128)S(1)}, f32[3,240,128]{2,1,0:T(8,128)S(1)}, u32[]{:S(2)}, u32[]{:S(2)}) collective-permute-start(f32[3,240,128]{2,1,0:T(8,128)S(1)} %add.194), channel_id=1, source_target_pairs={{0,64},{32,224},{64,128},{96,32},{128,192},{160,96},{192,0},{224,1... | collective-permute-start | bytes 1105928 | tf_op jit(solution)/shard_map/ppermute | solution.py:257
  35.0 3.2 %collective-permute-start.23 = (f32[8,144,128]{2,1,0:T(8,128)S(1)}, f32[8,144,128]{2,1,0:T(8,128)S(1)}, u32[]{:S(2)}, u32[]{:S(2)}) collective-permute-start(f32[8,144,128]{2,1,0:T(8,128)S(1)} %pad_maximum_fusion.2), channel_id=1, source_target_pairs={{0,4},{4,8},{8,12},{12,16},{16,20},{20,24},{24,28},{28,0},{32,60},... | collective-permute-start | bytes 1769480 | tf_op jit(solution)/shard_map/ppermute | solution.py:261
  39.5 3.3 %collective-permute-start.3 = (f32[5,240,128]{2,1,0:T(8,128)S(1)}, f32[5,240,128]{2,1,0:T(8,128)S(1)}, u32[]{:S(2)}, u32[]{:S(2)}) collective-permute-start(f32[5,240,128]{2,1,0:T(8,128)S(1)} %add.188), channel_id=1, source_target_pairs={{0,64},{32,224},{64,128},{96,32},{128,192},{160,96},{192,0},{224,1... | collective-permute-start | bytes 1843208 | tf_op jit(solution)/shard_map/ppermute | solution.py:257
  43.0 2.1 %collective-permute-done.23 = f32[8,144,128]{2,1,0:T(8,128)S(1)} collective-permute-done((f32[8,144,128]{2,1,0:T(8,128)S(1)}, f32[8,144,128]{2,1,0:T(8,128)S(1)}, u32[]{:S(2)}, u32[]{:S(2)}) %collective-permute-start.23) | collective-permute-done | bytes 589856 | tf_op jit(solution)/shard_map/ppermute | solution.py:261
  45.2 3.4 %collective-permute-start.24 = (f32[8,144,128]{2,1,0:T(8,128)S(1)}, f32[8,144,128]{2,1,0:T(8,128)S(1)}, u32[]{:S(2)}, u32[]{:S(2)}) collective-permute-start(f32[8,144,128]{2,1,0:T(8,128)S(1)} %add_add_fusion), channel_id=1, source_target_pairs={{0,4},{4,8},{8,12},{12,16},{16,20},{20,24},{24,28},{28,0},{32,60},... | collective-permute-start | bytes 1769480 | tf_op jit(solution)/shard_map/ppermute | solution.py:261
  50.1 3.2 %collective-permute-start.4 = (f32[10,240,128]{2,1,0:T(8,128)S(1)}, f32[10,240,128]{2,1,0:T(8,128)S(1)}, u32[]{:S(2)}, u32[]{:S(2)}) collective-permute-start(f32[10,240,128]{2,1,0:T(8,128)S(1)} %pad_maximum_fusion), channel_id=1, source_target_pairs={{0,64},{32,224},{64,128},{96,32},{128,192},{160,96},{192,0},{224,1... | collective-permute-start | bytes 3686408 | tf_op jit(solution)/shard_map/ppermute | solution.py:257
  55.0 2.7 %collective-permute-done.10 = f32[6,240,128]{2,1,0:T(8,128)S(1)} collective-permute-done((f32[6,240,128]{2,1,0:T(8,128)S(1)}, f32[6,240,128]{2,1,0:T(8,128)S(1)}, u32[]{:S(2)}, u32[]{:S(2)}) %collective-permute-start.10) | collective-permute-done | bytes 737312 | tf_op jit(solution)/shard_map/ppermute | solution.py:257
  57.8 4.8 %collective-permute-start.11 = (f32[3,240,128]{2,1,0:T(8,128)S(1)}, f32[3,240,128]{2,1,0:T(8,128)S(1)}, u32[]{:S(2)}, u32[]{:S(2)}) collective-permute-start(f32[3,240,128]{2,1,0:T(8,128)S(1)} %slice.396), channel_id=1, source_target_pairs={{0,32},{32,0},{64,96},{96,64},{128,160},{160,128},{192,224},{224,1... | collective-permute-start | bytes 1105928 | tf_op jit(solution)/shard_map/ppermute | solution.py:253
  66.4 5.5 %collective-permute-done.25 = f32[8,144,128]{2,1,0:T(8,128)S(1)} collective-permute-done((f32[8,144,128]{2,1,0:T(8,128)S(1)}, f32[8,144,128]{2,1,0:T(8,128)S(1)}, u32[]{:S(2)}, u32[]{:S(2)}) %collective-permute-start.25) | collective-permute-done | bytes 589856 | tf_op jit(solution)/shard_map/ppermute | solution.py:261
  71.9 2.2 %collective-permute-start.26 = (f32[4,144,128]{2,1,0:T(8,128)S(1)}, f32[4,144,128]{2,1,0:T(8,128)S(1)}, u32[]{:S(2)}, u32[]{:S(2)}) collective-permute-start(f32[4,144,128]{2,1,0:T(8,128)S(1)} %slice.422), channel_id=1, source_target_pairs={{0,32},{32,0},{64,96},{96,64},{128,160},{160,128},{192,224},{224,1... | collective-permute-start | bytes 884744 | tf_op jit(solution)/shard_map/ppermute | solution.py:253
  78.1 3.2 %collective-permute-done.13 = f32[2,240,128]{2,1,0:T(8,128)S(1)} collective-permute-done((f32[2,240,128]{2,1,0:T(8,128)S(1)}, f32[2,240,128]{2,1,0:T(8,128)S(1)}, u32[]{:S(2)}, u32[]{:S(2)}) %collective-permute-start.13) | collective-permute-done | bytes 245792 | tf_op jit(solution)/shard_map/ppermute | solution.py:261
  81.3 3.0 %collective-permute-start.14 = (f32[2,240,128]{2,1,0:T(8,128)S(1)}, f32[2,240,128]{2,1,0:T(8,128)S(1)}, u32[]{:S(2)}, u32[]{:S(2)}) collective-permute-start(f32[2,240,128]{2,1,0:T(8,128)S(1)} %pad_maximum_fusion.12), channel_id=1, source_target_pairs={{0,4},{4,8},{8,12},{12,16},{16,20},{20,24},{24,28},{28,0},{32,60},... | collective-permute-start | bytes 737288 | tf_op jit(solution)/shard_map/ppermute | solution.py:261
  84.5 3.0 %collective-permute-done.14 = f32[2,240,128]{2,1,0:T(8,128)S(1)} collective-permute-done((f32[2,240,128]{2,1,0:T(8,128)S(1)}, f32[2,240,128]{2,1,0:T(8,128)S(1)}, u32[]{:S(2)}, u32[]{:S(2)}) %collective-permute-start.14) | collective-permute-done | bytes 245792 | tf_op jit(solution)/shard_map/ppermute | solution.py:261
  87.6 3.2 %collective-permute-start.15 = (f32[2,240,128]{2,1,0:T(8,128)S(1)}, f32[2,240,128]{2,1,0:T(8,128)S(1)}, u32[]{:S(2)}, u32[]{:S(2)}) collective-permute-start(f32[2,240,128]{2,1,0:T(8,128)S(1)} %pad_maximum_fusion.13), channel_id=1, source_target_pairs={{0,4},{4,8},{8,12},{12,16},{16,20},{20,24},{24,28},{28,0},{32,60},... | collective-permute-start | bytes 737288 | tf_op jit(solution)/shard_map/ppermute | solution.py:261
  91.2 2.7 %collective-permute-done.15 = f32[2,240,128]{2,1,0:T(8,128)S(1)} collective-permute-done((f32[2,240,128]{2,1,0:T(8,128)S(1)}, f32[2,240,128]{2,1,0:T(8,128)S(1)}, u32[]{:S(2)}, u32[]{:S(2)}) %collective-permute-start.15) | collective-permute-done | bytes 245792 | tf_op jit(solution)/shard_map/ppermute | solution.py:261
  93.9 4.6 %collective-permute-start.16 = (f32[240,128]{1,0:T(8,128)S(1)}, f32[240,128]{1,0:T(8,128)S(1)}, u32[]{:S(2)}, u32[]{:S(2)}) collective-permute-start(f32[240,128]{1,0:T(8,128)S(1)} %slice_bitcast_fusion), channel_id=1, source_target_pairs={{0,32},{32,0},{64,96},{96,64},{128,160},{160,128},{192,224},{224,1... | collective-permute-start | bytes 368648 | tf_op jit(solution)/shard_map/ppermute | solution.py:253
  100.1 1.9 %collective-permute-start.30 = (f32[6,4,8,128]{3,0,2,1:T(8,128)S(1)}, f32[6,4,8,128]{3,0,2,1:T(8,128)S(1)}, u32[]{:S(2)}, u32[]{:S(2)}) collective-permute-start(f32[6,4,8,128]{3,0,2,1:T(8,128)S(1)} %get-tuple-element.45), channel_id=1, source_target_pairs={{32,64},{64,32},{96,128},{128,96},{160,192},{192,160},{33,65},{65,... | collective-permute-start | bytes 294920 | tf_op jit(solution)/shard_map/ppermute | solution.py:352
  102.0 4.3 %collective-permute-done.30 = f32[6,4,8,128]{3,0,2,1:T(8,128)S(1)} collective-permute-done((f32[6,4,8,128]{3,0,2,1:T(8,128)S(1)}, f32[6,4,8,128]{3,0,2,1:T(8,128)S(1)}, u32[]{:S(2)}, u32[]{:S(2)}) %collective-permute-start.30) | collective-permute-done | bytes 98336 | tf_op jit(solution)/shard_map/ppermute | solution.py:352
  108.0 4.0 %collective-permute-start.32 = (f32[6,8,4,128]{3,0,2,1:T(8,128)S(1)}, f32[6,8,4,128]{3,0,2,1:T(8,128)S(1)}, u32[]{:S(2)}, u32[]{:S(2)}) collective-permute-start(f32[6,8,4,128]{3,0,2,1:T(8,128)S(1)} %get-tuple-element.36), channel_id=1, source_target_pairs={{0,4},{4,8},{8,12},{12,16},{16,20},{20,24},{24,28},{1,5},{5,9},{9,... | collective-permute-start | bytes 294920 | tf_op jit(solution)/shard_map/ppermute | solution.py:290
  115.6 4.0 %collective-permute-start.34 = (f32[6,8,8,4]{3,0,2,1:T(8,128)S(1)}, f32[6,8,8,4]{3,0,2,1:T(8,128)S(1)}, u32[]{:S(2)}, u32[]{:S(2)}) collective-permute-start(f32[6,8,8,4]{3,0,2,1:T(8,128)S(1)} %get-tuple-element.34), channel_id=1, source_target_pairs={{0,1},{1,2},{2,3},{4,5},{5,6},{6,7},{8,9},{9,10},{10,11},{12,13},{... | collective-permute-start | bytes 18440 | tf_op jit(solution)/shard_map/ppermute | solution.py:290
  (108 shorter events, 31.0 us)
Async XLA Ops:
  18.2 20.1 %collective-permute-start.7 = (f32[6,240,128]{2,1,0:T(8,128)S(1)}, f32[6,240,128]{2,1,0:T(8,128)S(1)}, u32[]{:S(2)}, u32[]{:S(2)}) collective-permute-start(f32[6,240,128]{2,1,0:T(8,128)S(1)} %bitcast.61), channel_id=1, source_target_pairs={{0,32},{32,0},{64,96},{96,64},{128,160},{160,128},{192,224},{224,1... | collective-permute-start | bytes 2211848 | tf_op jit(solution)/shard_map/ppermute | solution.py:253
  21.4 7.9 %collective-permute-start.8 = (f32[3,240,128]{2,1,0:T(8,128)S(1)}, f32[3,240,128]{2,1,0:T(8,128)S(1)}, u32[]{:S(2)}, u32[]{:S(2)}) collective-permute-start(f32[3,240,128]{2,1,0:T(8,128)S(1)} %bitcast.68), channel_id=1, source_target_pairs={{0,32},{32,0},{64,96},{96,64},{128,160},{160,128},{192,224},{224,1... | collective-permute-start | bytes 1105928 | tf_op jit(solution)/shard_map/ppermute | solution.py:253
  21.7 13.3 %collective-permute-start.2 = (f32[5,240,128]{2,1,0:T(8,128)S(1)}, f32[5,240,128]{2,1,0:T(8,128)S(1)}, u32[]{:S(2)}, u32[]{:S(2)}) collective-permute-start(f32[5,240,128]{2,1,0:T(8,128)S(1)} %bitcast.63), channel_id=1, source_target_pairs={{0,32},{32,0},{64,96},{96,64},{128,160},{160,128},{192,224},{224,1... | collective-permute-start | bytes 1843208 | tf_op jit(solution)/shard_map/ppermute | solution.py:253
  22.7 6.8 %collective-permute-start.20 = (f32[8,144,128]{2,1,0:T(8,128)S(1)}, f32[8,144,128]{2,1,0:T(8,128)S(1)}, u32[]{:S(2)}, u32[]{:S(2)}) collective-permute-start(f32[8,144,128]{2,1,0:T(8,128)S(1)} %bitcast.66), channel_id=1, source_target_pairs={{0,32},{32,0},{64,96},{96,64},{128,160},{160,128},{192,224},{224,1... | collective-permute-start | bytes 1769480 | tf_op jit(solution)/shard_map/ppermute | solution.py:253
  25.0 7.8 %collective-permute-start.22 = (f32[4,144,128]{2,1,0:T(8,128)S(1)}, f32[4,144,128]{2,1,0:T(8,128)S(1)}, u32[]{:S(2)}, u32[]{:S(2)}) collective-permute-start(f32[4,144,128]{2,1,0:T(8,128)S(1)} %add.210), channel_id=1, source_target_pairs={{0,4},{4,8},{8,12},{12,16},{16,20},{20,24},{24,28},{28,0},{32,60},... | collective-permute-start | bytes 884744 | tf_op jit(solution)/shard_map/ppermute | solution.py:261
  29.3 19.3 %collective-permute-start.1 = (f32[10,240,128]{2,1,0:T(8,128)S(1)}, f32[10,240,128]{2,1,0:T(8,128)S(1)}, u32[]{:S(2)}, u32[]{:S(2)}) collective-permute-start(f32[10,240,128]{2,1,0:T(8,128)S(1)} %bitcast.58), channel_id=1, source_target_pairs={{0,32},{32,0},{64,96},{96,64},{128,160},{160,128},{192,224},{224,1... | collective-permute-start | bytes 3686408 | tf_op jit(solution)/shard_map/ppermute | solution.py:253
  29.5 13.4 %collective-permute-start.19 = (f32[8,144,128]{2,1,0:T(8,128)S(1)}, f32[8,144,128]{2,1,0:T(8,128)S(1)}, u32[]{:S(2)}, u32[]{:S(2)}) collective-permute-start(f32[8,144,128]{2,1,0:T(8,128)S(1)} %bitcast.65), channel_id=1, source_target_pairs={{0,32},{32,0},{64,96},{96,64},{128,160},{160,128},{192,224},{224,1... | collective-permute-start | bytes 1769480 | tf_op jit(solution)/shard_map/ppermute | solution.py:253
  32.8 6.7 %collective-permute-start.9 = (f32[3,240,128]{2,1,0:T(8,128)S(1)}, f32[3,240,128]{2,1,0:T(8,128)S(1)}, u32[]{:S(2)}, u32[]{:S(2)}) collective-permute-start(f32[3,240,128]{2,1,0:T(8,128)S(1)} %add.194), channel_id=1, source_target_pairs={{0,64},{32,224},{64,128},{96,32},{128,192},{160,96},{192,0},{224,1... | collective-permute-start | bytes 1105928 | tf_op jit(solution)/shard_map/ppermute | solution.py:257
  35.0 10.0 %collective-permute-start.23 = (f32[8,144,128]{2,1,0:T(8,128)S(1)}, f32[8,144,128]{2,1,0:T(8,128)S(1)}, u32[]{:S(2)}, u32[]{:S(2)}) collective-permute-start(f32[8,144,128]{2,1,0:T(8,128)S(1)} %pad_maximum_fusion.2), channel_id=1, source_target_pairs={{0,4},{4,8},{8,12},{12,16},{16,20},{20,24},{24,28},{28,0},{32,60},... | collective-permute-start | bytes 1769480 | tf_op jit(solution)/shard_map/ppermute | solution.py:261
  38.3 24.3 %collective-permute-start.18 = (f32[8,144,128]{2,1,0:T(8,128)S(1)}, f32[8,144,128]{2,1,0:T(8,128)S(1)}, u32[]{:S(2)}, u32[]{:S(2)}) collective-permute-start(f32[8,144,128]{2,1,0:T(8,128)S(1)} %bitcast.64), channel_id=1, source_target_pairs={{0,32},{32,0},{64,96},{96,64},{128,160},{160,128},{192,224},{224,1... | collective-permute-start | bytes 1769480 | tf_op jit(solution)/shard_map/ppermute | solution.py:253
  39.5 10.4 %collective-permute-start.3 = (f32[5,240,128]{2,1,0:T(8,128)S(1)}, f32[5,240,128]{2,1,0:T(8,128)S(1)}, u32[]{:S(2)}, u32[]{:S(2)}) collective-permute-start(f32[5,240,128]{2,1,0:T(8,128)S(1)} %add.188), channel_id=1, source_target_pairs={{0,64},{32,224},{64,128},{96,32},{128,192},{160,96},{192,0},{224,1... | collective-permute-start | bytes 1843208 | tf_op jit(solution)/shard_map/ppermute | solution.py:257
  42.9 14.9 %collective-permute-start.10 = (f32[6,240,128]{2,1,0:T(8,128)S(1)}, f32[6,240,128]{2,1,0:T(8,128)S(1)}, u32[]{:S(2)}, u32[]{:S(2)}) collective-permute-start(f32[6,240,128]{2,1,0:T(8,128)S(1)} %pad_maximum_fusion.1), channel_id=1, source_target_pairs={{0,64},{32,224},{64,128},{96,32},{128,192},{160,96},{192,0},{224,1... | collective-permute-start | bytes 2211848 | tf_op jit(solution)/shard_map/ppermute | solution.py:257
  45.2 17.4 %collective-permute-start.24 = (f32[8,144,128]{2,1,0:T(8,128)S(1)}, f32[8,144,128]{2,1,0:T(8,128)S(1)}, u32[]{:S(2)}, u32[]{:S(2)}) collective-permute-start(f32[8,144,128]{2,1,0:T(8,128)S(1)} %add_add_fusion), channel_id=1, source_target_pairs={{0,4},{4,8},{8,12},{12,16},{16,20},{20,24},{24,28},{28,0},{32,60},... | collective-permute-start | bytes 1769480 | tf_op jit(solution)/shard_map/ppermute | solution.py:261
  50.1 24.0 %collective-permute-start.4 = (f32[10,240,128]{2,1,0:T(8,128)S(1)}, f32[10,240,128]{2,1,0:T(8,128)S(1)}, u32[]{:S(2)}, u32[]{:S(2)}) collective-permute-start(f32[10,240,128]{2,1,0:T(8,128)S(1)} %pad_maximum_fusion), channel_id=1, source_target_pairs={{0,64},{32,224},{64,128},{96,32},{128,192},{160,96},{192,0},{224,1... | collective-permute-start | bytes 3686408 | tf_op jit(solution)/shard_map/ppermute | solution.py:257
  53.3 11.3 %collective-permute-start.6 = (f32[3,240,128]{2,1,0:T(8,128)S(1)}, f32[3,240,128]{2,1,0:T(8,128)S(1)}, u32[]{:S(2)}, u32[]{:S(2)}) collective-permute-start(f32[3,240,128]{2,1,0:T(8,128)S(1)} %bitcast.67), channel_id=1, source_target_pairs={{0,32},{32,0},{64,96},{96,64},{128,160},{160,128},{192,224},{224,1... | collective-permute-start | bytes 1105928 | tf_op jit(solution)/shard_map/ppermute | solution.py:253
  57.8 6.8 %collective-permute-start.11 = (f32[3,240,128]{2,1,0:T(8,128)S(1)}, f32[3,240,128]{2,1,0:T(8,128)S(1)}, u32[]{:S(2)}, u32[]{:S(2)}) collective-permute-start(f32[3,240,128]{2,1,0:T(8,128)S(1)} %slice.396), channel_id=1, source_target_pairs={{0,32},{32,0},{64,96},{96,64},{128,160},{160,128},{192,224},{224,1... | collective-permute-start | bytes 1105928 | tf_op jit(solution)/shard_map/ppermute | solution.py:253
  62.7 9.1 %collective-permute-start.25 = (f32[8,144,128]{2,1,0:T(8,128)S(1)}, f32[8,144,128]{2,1,0:T(8,128)S(1)}, u32[]{:S(2)}, u32[]{:S(2)}) collective-permute-start(f32[8,144,128]{2,1,0:T(8,128)S(1)} %add_add_fusion.1), channel_id=1, source_target_pairs={{0,4},{4,8},{8,12},{12,16},{16,20},{20,24},{24,28},{28,0},{32,60},... | collective-permute-start | bytes 1769480 | tf_op jit(solution)/shard_map/ppermute | solution.py:261
  64.7 11.1 %collective-permute-start.12 = (f32[1,240,128]{2,1,0:T(8,128)S(1)}, f32[1,240,128]{2,1,0:T(8,128)S(1)}, u32[]{:S(2)}, u32[]{:S(2)}) collective-permute-start(f32[1,240,128]{2,1,0:T(8,128)S(1)} %slice.398), channel_id=1, source_target_pairs={{0,4},{4,8},{8,12},{12,16},{16,20},{20,24},{24,28},{28,0},{32,60},... | collective-permute-start | bytes 368648 | tf_op jit(solution)/shard_map/ppermute | solution.py:261
  65.8 12.0 %collective-permute-start = (f32[5,240,128]{2,1,0:T(8,128)S(1)}, f32[5,240,128]{2,1,0:T(8,128)S(1)}, u32[]{:S(2)}, u32[]{:S(2)}) collective-permute-start(f32[5,240,128]{2,1,0:T(8,128)S(1)} %bitcast.62), channel_id=1, source_target_pairs={{0,32},{32,0},{64,96},{96,64},{128,160},{160,128},{192,224},{224,1... | collective-permute-start | bytes 1843208 | tf_op jit(solution)/shard_map/ppermute | solution.py:253
  65.8 11.8 %collective-permute-start.17 = (f32[4,144,128]{2,1,0:T(8,128)S(1)}, f32[4,144,128]{2,1,0:T(8,128)S(1)}, u32[]{:S(2)}, u32[]{:S(2)}) collective-permute-start(f32[4,144,128]{2,1,0:T(8,128)S(1)} %bitcast.69), channel_id=1, source_target_pairs={{0,32},{32,0},{64,96},{96,64},{128,160},{160,128},{192,224},{224,1... | collective-permute-start | bytes 884744 | tf_op jit(solution)/shard_map/ppermute | solution.py:253
  77.8 6.6 %collective-permute-start.27 = (f32[1,144,128]{2,1,0:T(8,128)S(1)}, f32[1,144,128]{2,1,0:T(8,128)S(1)}, u32[]{:S(2)}, u32[]{:S(2)}) collective-permute-start(f32[1,144,128]{2,1,0:T(8,128)S(1)} %slice.425), channel_id=1, source_target_pairs={{0,64},{32,224},{64,128},{96,32},{128,192},{160,96},{192,0},{224,1... | collective-permute-start | bytes 221192 | tf_op jit(solution)/shard_map/ppermute | solution.py:257
  90.8 7.8 %collective-permute-start.29 = (f32[144,128]{1,0:T(8,128)S(1)}, f32[144,128]{1,0:T(8,128)S(1)}, u32[]{:S(2)}, u32[]{:S(2)}) collective-permute-start(f32[144,128]{1,0:T(8,128)S(1)} %slice_bitcast_fusion.1), channel_id=1, source_target_pairs={{0,32},{32,0},{64,96},{96,64},{128,160},{160,128},{192,224},{224,1... | collective-permute-start | bytes 221192 | tf_op jit(solution)/shard_map/ppermute | solution.py:253
  114.3 7.1 %collective-permute-start.35 = (f32[6,8,8,4]{3,0,2,1:T(8,128)S(1)}, f32[6,8,8,4]{3,0,2,1:T(8,128)S(1)}, u32[]{:S(2)}, u32[]{:S(2)}) collective-permute-start(f32[6,8,8,4]{3,0,2,1:T(8,128)S(1)} %get-tuple-element.35), channel_id=1, source_target_pairs={{1,0},{2,1},{3,2},{5,4},{6,5},{7,6},{9,8},{10,9},{11,10},{13,12},{... | collective-permute-start | bytes 18440 | tf_op jit(solution)/shard_map/ppermute | solution.py:293
  115.6 7.3 %collective-permute-start.34 = (f32[6,8,8,4]{3,0,2,1:T(8,128)S(1)}, f32[6,8,8,4]{3,0,2,1:T(8,128)S(1)}, u32[]{:S(2)}, u32[]{:S(2)}) collective-permute-start(f32[6,8,8,4]{3,0,2,1:T(8,128)S(1)} %get-tuple-element.34), channel_id=1, source_target_pairs={{0,1},{1,2},{2,3},{4,5},{5,6},{6,7},{8,9},{9,10},{10,11},{12,13},{... | collective-permute-start | bytes 18440 | tf_op jit(solution)/shard_map/ppermute | solution.py:290
  (12 other events, 62.4 us)

commit v3 on v2

--- a/solution.py
+++ b/solution.py
@@ -1,3 +1,4 @@
+import functools
 import math
 
 import jax
@@ -45,7 +46,7 @@
 
 
 def block_tables():
-    table = np.zeros((2 * CHIPS, LON, 2, 2 * CHIPS * LON), np.int32)
+    table = np.zeros((2 * CHIPS, LON, 8, 128), np.int32)
     for lat in range(2 * CHIPS):
         for z in range(LON):
             for owner in range(2 * CHIPS * LON):
@@ -64,7 +65,7 @@
                     table[lat, z, half, owner] = GY * (
                         64 * COLS[0] * half + block * COLS[half]
                     )
-    return table
+    return table.reshape(2 * CHIPS * LON, 8, 128)
 
 
 def project_kernel(
@@ -73,7 +74,8 @@
     owner_ref,
     column_ref,
     basis_ref,
-    table_ref,
+    me_ref,
+    tables_ref,
     acc,
     raw,
     plain,
@@ -84,6 +86,7 @@
     pos_s,
     row_s,
     end_s,
+    table_s,
     raw_sems,
     sems,
 ):
@@ -92,6 +95,8 @@
     channels, elems, _ = kernels_ref.shape
     pitch = plain.shape[0] // channels
 
+    table = pltpu.make_async_copy(tables_ref.at[me_ref[0]], table_s, sems.at[3])
+    table.start()
     fetches = [
         pltpu.make_async_copy(kernels_ref.at[c], raw.at[c], raw_sems.at[c])
         for c in range(channels)
@@ -99,40 +104,47 @@
     for fetch in fetches:
         fetch.start()
 
+    basis = basis_ref[...]
+    hits = [basis == b for b in range(basis_count)]
+    upper = (
+        lax.broadcasted_iota(jnp.int32, (lanes, lanes), 0)
+        <= lax.broadcasted_iota(jnp.int32, (lanes, lanes), 1)
+    ).astype(jnp.float32)
+    every = basis_count * rows
+    to = lax.broadcasted_iota(jnp.int32, (every, every), 0)
+    source = lax.broadcasted_iota(jnp.int32, (every, every), 1)
+    lower = ((source < to) & (source // rows == to // rows)).astype(jnp.float32)
+    inside = jnp.dot(
+        jnp.concatenate([hit.astype(jnp.float32) for hit in hits]),
+        upper,
+        preferred_element_type=jnp.float32,
+    )
+    in_row = jnp.broadcast_to(inside[:, lanes - 1 :], (every, lanes))
+    before = jnp.dot(lower, in_row, preferred_element_type=jnp.float32)
+    ranks = (before + inside).astype(jnp.int32) - 1
+    totals = (before + in_row).astype(jnp.int32)
+    base = jnp.zeros((1, lanes), jnp.int32)
+    pos = jnp.zeros((rows, lanes), jnp.int32)
+    for b, hit in enumerate(hits):
+        end = (b + 1) * rows
+        pos = jnp.where(hit, base + ranks[end - rows : end], pos)
+        base = base + (totals[end - 1 : end] + CHUNK - 1) // CHUNK * CHUNK
+        end_v[pl.ds(b, 1), :] = base // CHUNK
+    pos_v[...] = pos * channels
+
     owner = owner_ref[...]
     column = column_ref[...]
     first = jnp.zeros((rows, lanes), jnp.int32)
     second = jnp.zeros((rows, lanes), jnp.int32)
-    for o in range(table_ref.shape[1]):
+    table.wait()
+    for o in range(2 * CHIPS * LON):
         hit = owner == o
-        first = jnp.where(hit, table_ref[0, o], first)
-        second = jnp.where(hit, table_ref[1, o], second)
+        first = jnp.where(hit, table_s[0, o], first)
+        second = jnp.where(hit, table_s[1, o], second)
     width = GY * COLS[0]
     row = jnp.where(column < width, first + column, second + column - width)
     row_v[...] = row * channels
 
-    basis = basis_ref[...]
-    upper = (
-        lax.broadcasted_iota(jnp.int32, (lanes, lanes), 0)
-        <= lax.broadcasted_iota(jnp.int32, (lanes, lanes), 1)
-    ).astype(jnp.float32)
-    lower = (
-        lax.broadcasted_iota(jnp.int32, (rows, rows), 1)
-        < lax.broadcasted_iota(jnp.int32, (rows, rows), 0)
-    ).astype(jnp.float32)
-    base = jnp.zeros((1, lanes), jnp.int32)
-    pos = jnp.zeros((rows, lanes), jnp.int32)
-    for b in range(basis_count):
-        hit = basis == b
-        inside = jnp.dot(hit.astype(jnp.float32), upper, preferred_element_type=jnp.float32)
-        in_row = jnp.broadcast_to(inside[:, lanes - 1 :], (rows, lanes))
-        before = jnp.dot(lower, in_row, preferred_element_type=jnp.float32)
-        rank = (before + inside).astype(jnp.int32) - 1
-        total = (before + in_row)[rows - 1 :].astype(jnp.int32)
-        pos = jnp.where(hit, base + rank, pos)
-        base = base + (total + CHUNK - 1) // CHUNK * CHUNK
-        end_v[pl.ds(b, 1), :] = base // CHUNK
-    pos_v[...] = pos * channels
     loads = [
         pltpu.make_async_copy(source, target, sems.at[i])
         for i, (source, target) in enumerate(
@@ -202,7 +214,7 @@
     lax.fori_loop(0, rows, scatter, 0)
 
 
-def project(kernels, basis_weights, owner, column, basis, table):
+def project(kernels, basis_weights, owner, column, basis, me, tables):
     elems, channels, points = kernels.shape
     rows = elems // 128
     room = elems + 8 * CHUNK
@@ -214,7 +226,7 @@
         out_shape=pltpu.VMEM((total, 128), jnp.float32),
         in_specs=[pl.BlockSpec(memory_space=pl.ANY)]
         + [vmem] * 4
-        + [pl.BlockSpec(memory_space=pltpu.SMEM)],
+        + [pl.BlockSpec(memory_space=pltpu.SMEM), pl.BlockSpec(memory_space=pl.ANY)],
         out_specs=vmem,
         scratch_shapes=[
             pltpu.VMEM((channels, elems, 128), jnp.bfloat16),
@@ -226,8 +238,9 @@
             pltpu.SMEM((rows, 128), jnp.int32),
             pltpu.SMEM((rows, 128), jnp.int32),
             pltpu.SMEM((8, 128), jnp.int32),
+            pltpu.SMEM((8, 128), jnp.int32),
             pltpu.SemaphoreType.DMA((channels,)),
-            pltpu.SemaphoreType.DMA((3,)),
+            pltpu.SemaphoreType.DMA((4,)),
         ],
         compiler_params=pltpu.CompilerParams(vmem_limit_bytes=48 * 1024 * 1024),
         name="project",
@@ -237,16 +250,21 @@
         owner.reshape(rows, 128),
         column.reshape(rows, 128),
         basis.reshape(rows, 128),
-        table,
-    )
-    parts = []
+        me,
+        tables,
+    )
+    return acc
+
+
+def part_rows(channels):
+    found = []
     start = 0
-    for counts, cols in ((PARTS_A * 2, COLS[0]), (PARTS_B * 2, COLS[1])):
-        size = cols * GY * channels
-        for count in counts:
-            parts.append(acc[start : start + count * size].reshape(count, size, 128))
-            start += count * size
-    return parts
+    for counts, cols in ((PARTS_A, COLS[0]), (PARTS_B, COLS[1])):
+        for _ in range(2):
+            rows = [count * cols * GY * channels for count in counts]
+            found.append([(start + sum(rows[:i]), rows[i]) for i in range(len(rows))])
+            start += sum(rows)
+    return found
 
 
 def over_core(value):
@@ -264,6 +282,10 @@
 def add_at(block, part, start):
     end = start + part.shape[0]
     return jnp.concatenate([block[:start], block[start:end] + part, block[end:]])
+
+
+def after(value, *others):
+    return lax.optimization_barrier((value, others))[0]
 
 
 def gauss_taps():
@@ -283,60 +305,90 @@
     return result
 
 
-def with_halo(block, axis, dim, width):
-    count = lax.axis_size(axis)
-    forward = [(i, i + 1) for i in range(count - 1)]
-    backward = [(target, source) for source, target in forward]
-    low = lax.ppermute(
-        lax.slice_in_dim(block, block.shape[dim] - width, None, axis=dim), axis, forward
-    )
-    high = lax.ppermute(lax.slice_in_dim(block, 0, width, axis=dim), axis, backward)
-    return jnp.concatenate([low, block, high], axis=dim)
+def steps_along(count):
+    pairs = []
+    for lat in range(2 * CHIPS):
+        for i in range(count):
+            j = i + 1 - 2 * (lat % 2)
+            if 0 <= j < count:
+                pairs.append((lat * count + i, lat * count + j))
+    return pairs
+
+
+def halos(low, high, axis, even):
+    other = over_core(jnp.where(even, low, high))
+    came = lax.ppermute(
+        jnp.stack([jnp.where(even, high, low), other]),
+        ("lat", axis),
+        steps_along(lax.axis_size(axis)),
+    )
+    other = over_core(came[1])
+    return jnp.where(even, came[0], other), jnp.where(even, other, came[0])
+
+
+def depth_taps(cells):
+    taps = np.zeros((cells + 2 * RADIUS, cells), np.float32)
+    for cell in range(cells):
+        taps[cell : cell + 2 * RADIUS + 1, cell] = gauss_taps()
+    return taps
 
 
 def local(kernels, basis_weights, owner_block, column_offset, basis_index):
     lat = lax.axis_index("lat")
     lon = lax.axis_index("lon")
-    table = lax.dynamic_slice(
-        jnp.asarray(block_tables()), (lat, lon, 0, 0), (1, 1, 2, 64)
-    ).reshape(2, 64)
-    parts = project(
-        kernels, basis_weights, owner_block, column_offset, basis_index, table
-    )
-    keep_a, send_a = parts[0:6], parts[6:12]
-    keep_b, send_b = parts[12:17], parts[17:22]
-
-    p2 = [keep_a[0] + over_core(send_a[0]), None]
-    q4 = keep_b[0] + over_core(send_b[0])
-    z_in = over_z(q4)
-    x_in = [over_x(p2[0]), None]
-    p2[1] = keep_a[1] + over_core(send_a[1])
-    x_in[1] = over_x(p2[1])
-    p1 = [keep_a[2 + i] + over_core(send_a[2 + i]) for i in range(2)]
-    q3 = keep_b[1] + over_core(send_b[1])
-    q2 = keep_b[2] + over_core(send_b[2])
-    q1 = keep_b[3] + over_core(send_b[3])
-    p0 = [keep_a[4 + i] + over_core(send_a[4 + i]) for i in range(2)]
-    q0 = keep_b[4] + over_core(send_b[4])
-
-    x_in[0] = over_x(add_at(p1[0], x_in[0], 1))
-    z_in = over_z(add_at(q3, z_in, 1))
-    x_in[1] = over_x(add_at(p1[1], x_in[1], 2))
-    z_in = over_z(q2 + z_in)
-    near = p0[0] + x_in[0][:3] + over_core(x_in[0][3:])
-    v = over_z(near[2:])
-    z_in = over_z(q1 + z_in)
-    v = over_z(jnp.concatenate([near[1:2] + v, near[:1]]))
-    far = p0[1] + x_in[1][:5] + over_core(x_in[1][5:])
-    v = over_z(jnp.concatenate([far[4:] + v[:1], far[:1] + v[1:]]))
-    b = q0 + z_in[:4] + over_core(z_in[4:])
-    w = over_x(b[3:])
-    v = over_z(jnp.concatenate([far[3:4] + v[:1], far[1:2] + v[1:]]))
-    w = over_x(jnp.concatenate([b[2:3] + w, b[:1]]))
-    final_a = far[2] + v[0] + over_core(v[1])
-    final_b = b[1] + w[0] + over_core(w[1])
-
     channels = kernels.shape[1]
+    acc = project(
+        kernels, basis_weights, owner_block, column_offset, basis_index,
+        (lat * LON + lon).reshape(1), jnp.asarray(block_tables()),
+    )
+    ra, rb = (cols * GY * channels for cols in COLS)
+    keep_a, send_a, keep_b, send_b = part_rows(channels)
+
+    def span(parts):
+        return acc[parts[0][0] : parts[-1][0] + parts[-1][1]]
+
+    def merged(keep, send, *steps):
+        value = span(send)
+        return span(keep) + over_core(after(value, *steps) if steps else value)
+
+    def met(mine, came, rows):
+        return mine + came[:rows] + over_core(came[rows:])
+
+    q = merged(keep_b[:1], send_b[:1])
+    p2 = [merged(keep_a[i : i + 1], send_a[i : i + 1]) for i in range(2)]
+    x = [over_x(part) for part in p2]
+    z = over_z(q)
+    p1 = merged(keep_a[2:3], send_a[2:3], q, *p2)
+    q3 = merged(keep_b[1:2], send_b[1:2], q, *p2)
+    rest_a = merged(keep_a[3:], send_a[3:], p1, q3)
+    rest_b = merged(keep_b[2:], send_b[2:], p1, q3)
+
+    step = add_at(p1, x[0], ra)
+    x[0] = over_x(step)
+    step = add_at(q3, z, rb)
+    z = over_z(step)
+    step = add_at(rest_a[: 10 * ra], x[1], 2 * ra)
+    x[1] = over_x(step)
+    step = rest_b[: 8 * rb] + z
+    z = over_z(step)
+    near = met(rest_a[10 * ra : 13 * ra], x[0], 3 * ra)
+    v = over_z(near[2 * ra :])
+    step = jnp.concatenate([near[ra : 2 * ra] + v, near[:ra]])
+    v = over_z(step)
+    step = rest_b[8 * rb : 16 * rb] + after(z, step)
+    z = over_z(step)
+    far = met(rest_a[13 * ra :], after(x[1], v), 5 * ra)
+    step = jnp.concatenate([far[4 * ra :], far[:ra]]) + v
+    v = over_z(step)
+    b = met(rest_b[16 * rb :], z, 4 * rb)
+    w = over_x(b[3 * rb :])
+    step = jnp.concatenate([far[3 * ra : 4 * ra], far[ra : 2 * ra]]) + v
+    v = over_z(step)
+    step = jnp.concatenate([b[2 * rb : 3 * rb] + w, b[:rb]])
+    w = over_x(step)
+    final_a = far[2 * ra : 3 * ra] + v[:ra] + over_core(v[ra:])
+    final_b = b[rb : 2 * rb] + w[:rb] + over_core(w[rb:])
+
     final_a = jnp.transpose(final_a.reshape(COLS[0], GY, channels, 128), (2, 0, 1, 3))
     final_b = jnp.transpose(final_b.reshape(COLS[1], GY, channels, 128), (2, 0, 1, 3))
     projected = jnp.concatenate([final_a, final_b], axis=1)
@@ -357,8 +409,22 @@
         ),
         1,
     )
-    along_lon = pass_along(with_halo(along_lat, "lon", 2, RADIUS), 2)
-    smoothed = pass_along(with_halo(along_lon, "dep", 3, RADIUS), 3)
+    low, high = halos(along_lat[:, :, :RADIUS], along_lat[:, :, GY - RADIUS :], "lon", even)
+    along_lon = pass_along(jnp.concatenate([low, along_lat, high], axis=2), 2)
+    flat = along_lon.reshape(channels * GX * GY, -1)
+    cells = flat.shape[1]
+    low, high = halos(
+        jnp.transpose(flat[:, :RADIUS]), jnp.transpose(flat[:, cells - RADIUS :]), "dep", even
+    )
+    taps = depth_taps(cells)
+    inside = jnp.dot(flat, taps[RADIUS : RADIUS + cells], precision=lax.Precision.HIGHEST)
+    outside = lax.dot_general(
+        jnp.concatenate([low, high]),
+        np.concatenate([taps[:RADIUS], taps[RADIUS + cells :]]),
+        (((0,), (0,)), ((), ())),
+        precision=lax.Precision.HIGHEST,
+    )
+    smoothed = (inside + outside).reshape(along_lon.shape)
     return (projected, smoothed)
 
 

time: 126 us -> 121 us (0.960)
  starting transfers between devices: 64.7 us -> 47.7 us
  waiting for transfers between devices: 35.5 us -> 50 us
  local copies, waits for them, and re-layouts: 3.88 us -> 1.61 us
  matrix products: 0 us -> 1.99 us
  Pallas kernels: 16.2 us -> 14.8 us
    ppermute x4 -> x2, starting transfers between devices: 10.6 us -> 2.6 us  [halos(): lax.ppermute(jnp.stack([jnp.where(even, high, low), other]), ('lat', axis...]
    ppermute x17, waiting for transfers between devices: 2.7 us -> 10.5 us  [over_core(): return lax.ppermute(value, 'lat', CORE)]
    ppermute x8, starting transfers between devices: 21.7 us -> 17.1 us  [over_z(): return lax.ppermute(value, ('lat', 'lon'), RING_Z)]
    ppermute x17, starting transfers between devices: 21.7 us -> 17.5 us  [over_core(): return lax.ppermute(value, 'lat', CORE)]
    ppermute x4 -> x2, waiting for transfers between devices: 4.49 us -> 8.28 us  [halos(): lax.ppermute(jnp.stack([jnp.where(even, high, low), other]), ('lat', axis...]
    ppermute x6, waiting for transfers between devices: 4.78 us -> 7.97 us  [over_x(): return lax.ppermute(value, 'lat', RING_X)]
    dot_general x0 -> x3, matrix products: none -> 1.99 us  [the longest x2 1.68 us: local(): lax.dot_general(jnp.concatenate([low, high]), np.concatenate([taps[:RADIU...]
    ppermute x6, starting transfers between devices: 8.79 us -> 7.13 us  [over_x(): return lax.ppermute(value, 'lat', RING_X)]
  transfers between devices with their start and end apart: 36 -> 34, of which waited for: 16 -> 21; matrix products, arithmetic and copies ran while one was open for 3% -> 3% of each run, Pallas kernels for 0% -> 0%
where the time goes in v3:
time: 121 us; the launch traced here: 120 us
  waiting for transfers between devices  50 us (41%)
  starting transfers between devices  47.7 us (39%)
  Pallas kernels  14.8 us (12%)
  other arithmetic  2.37 us (2%)
  matrix products  1.99 us (2%)
  local copies, waits for them, and re-layouts  1.61 us (1%)
    ppermute x8, waiting for transfers between devices, over_z(): return lax.ppermute(value, ('lat', 'lon'), RING_Z)  20.3 us
    ppermute x17, starting transfers between devices, over_core(): return lax.ppermute(value, 'lat', CORE)  17.5 us
    ppermute x8, starting transfers between devices, over_z(): return lax.ppermute(value, ('lat', 'lon'), RING_Z)  17.1 us
    pallas_call x1, Pallas kernels, project(): pl.pallas_call(project_kernel, out_shape=pltpu.VMEM((total, 128), jnp.flo...  14.8 us
    ppermute x17, waiting for transfers between devices, over_core(): return lax.ppermute(value, 'lat', CORE)  10.5 us
    ppermute x2, waiting for transfers between devices, halos(): lax.ppermute(jnp.stack([jnp.where(even, high, low), other]), ('lat', axis...  8.28 us
    ppermute x6, waiting for transfers between devices, over_x(): return lax.ppermute(value, 'lat', RING_X)  7.97 us
    ppermute x6, starting transfers between devices, over_x(): return lax.ppermute(value, 'lat', RING_X)  7.13 us
  transfers between devices with their start and end apart: 34, of which 21 were waited for; matrix products, arithmetic and copies ran while one was open for 3% of the time, Pallas kernels for 0%

profile of v3, /device:TPU:1, one launch (start us, length us, event | category | flops | bytes accessed | tf_op | source)
XLA Modules:
  0.0 119.6 jit_solution(12046638231976732947)
XLA Ops:
  0.6 14.8 %project.1 = f32[24576,128]{1,0:T(8,128)S(1)} custom-call(bf16[6,2048,128]{2,1,0:T(8,128)(2,1)} %bitcast.44, bf16[8,128,128]{2,1,0:T(8,128)(2,1)} %weights_ref.1, s32[16,128]{1,0:T(8,128)} %bitcast.53, s32[16,128]{1,0:T(8,128)} %bitcast.54, s32[16,128]{1,0:T(8,128)} %bitcast.55, s32[1]{0:T(128)} %bitcast.4.me_ref, s32[64,8,128]{2,1,0:T(8,128)} %constant.42.clone.tables_ref), custom_call_target="tpu_custom_call" | custom-call | tf_op jit(solution)/shard_map/project/pallas_call | solution.py:224
  15.5 3.3 %collective-permute-start = (f32[576,128]{1,0:T(8,128)S(1)}, f32[576,128]{1,0:T(8,128)S(1)}, u32[]{:S(2)}, u32[]{:S(2)}) collective-permute-start(f32[576,128]{1,0:T(8,128)S(1)} %slice.333), channel_id=1, source_target_pairs={{0,32},{32,0},{64,96},{96,64},{128,160},{160,128},{192,224},{224,1... | collective-permute-start | bytes 884744 | tf_op jit(solution)/shard_map/ppermute | solution.py:271
  25.3 3.9 %collective-permute-start.18 = (f32[576,128]{1,0:T(8,128)S(1)}, f32[576,128]{1,0:T(8,128)S(1)}, u32[]{:S(2)}, u32[]{:S(2)}) collective-permute-start(f32[576,128]{1,0:T(8,128)S(1)} %slice_add_fusion.14), channel_id=1, source_target_pairs={{0,4},{4,8},{8,12},{12,16},{16,20},{20,24},{24,28},{28,0},{32,60},... | collective-permute-start | bytes 884744 | tf_op jit(solution)/shard_map/ppermute | solution.py:279
  29.5 2.4 %collective-permute-start.9 = (f32[1440,128]{1,0:T(8,128)S(1)}, f32[1440,128]{1,0:T(8,128)S(1)}, u32[]{:S(2)}, u32[]{:S(2)}) collective-permute-start(f32[1440,128]{1,0:T(8,128)S(1)} %pad_maximum_fusion.1), channel_id=1, source_target_pairs={{0,64},{32,224},{64,128},{96,32},{128,192},{160,96},{192,0},{224,1... | collective-permute-start | bytes 2211848 | tf_op jit(solution)/shard_map/ppermute | solution.py:275
  33.0 3.7 %collective-permute-start.19 = (f32[1152,128]{1,0:T(8,128)S(1)}, f32[1152,128]{1,0:T(8,128)S(1)}, u32[]{:S(2)}, u32[]{:S(2)}) collective-permute-start(f32[1152,128]{1,0:T(8,128)S(1)} %pad_maximum_fusion.2), channel_id=1, source_target_pairs={{0,4},{4,8},{8,12},{12,16},{16,20},{20,24},{24,28},{28,0},{32,60},... | collective-permute-start | bytes 1769480 | tf_op jit(solution)/shard_map/ppermute | solution.py:279
  36.7 3.6 %collective-permute-done.9 = f32[1440,128]{1,0:T(8,128)S(1)} collective-permute-done((f32[1440,128]{1,0:T(8,128)S(1)}, f32[1440,128]{1,0:T(8,128)S(1)}, u32[]{:S(2)}, u32[]{:S(2)}) %collective-permute-start.9) | collective-permute-done | bytes 737312 | tf_op jit(solution)/shard_map/ppermute | solution.py:275
  40.3 4.2 %collective-permute-start.10 = (f32[720,128]{1,0:T(8,128)S(1)}, f32[720,128]{1,0:T(8,128)S(1)}, u32[]{:S(2)}, u32[]{:S(2)}) collective-permute-start(f32[720,128]{1,0:T(8,128)S(1)} %slice.349), channel_id=1, source_target_pairs={{0,32},{32,0},{64,96},{96,64},{128,160},{160,128},{192,224},{224,1... | collective-permute-start | bytes 1105928 | tf_op jit(solution)/shard_map/ppermute | solution.py:271
  44.7 3.9 %collective-permute-start.20 = (f32[1152,128]{1,0:T(8,128)S(1)}, f32[1152,128]{1,0:T(8,128)S(1)}, u32[]{:S(2)}, u32[]{:S(2)}) collective-permute-start(f32[1152,128]{1,0:T(8,128)S(1)} %slice_add_fusion.6), channel_id=1, source_target_pairs={{0,4},{4,8},{8,12},{12,16},{16,20},{20,24},{24,28},{28,0},{32,60},... | collective-permute-start | bytes 1769480 | tf_op jit(solution)/shard_map/ppermute | solution.py:279
  50.3 6.5 %collective-permute-done.11 = f32[240,128]{1,0:T(8,128)S(1)} collective-permute-done((f32[240,128]{1,0:T(8,128)S(1)}, f32[240,128]{1,0:T(8,128)S(1)}, u32[]{:S(2)}, u32[]{:S(2)}) %collective-permute-start.11) | collective-permute-done | bytes 122912 | tf_op jit(solution)/shard_map/ppermute | solution.py:279
  56.9 3.5 %collective-permute-start.21 = (f32[1152,128]{1,0:T(8,128)S(1)}, f32[1152,128]{1,0:T(8,128)S(1)}, u32[]{:S(2)}, u32[]{:S(2)}) collective-permute-start(f32[1152,128]{1,0:T(8,128)S(1)} %slice_add_fusion.7), channel_id=1, source_target_pairs={{0,4},{4,8},{8,12},{12,16},{16,20},{20,24},{24,28},{28,0},{32,60},... | collective-permute-start | bytes 1769480 | tf_op jit(solution)/shard_map/ppermute | solution.py:279
  60.5 9.4 %collective-permute-done.12 = f32[480,128]{1,0:T(8,128)S(1)} collective-permute-done((f32[480,128]{1,0:T(8,128)S(1)}, f32[480,128]{1,0:T(8,128)S(1)}, u32[]{:S(2)}, u32[]{:S(2)}) %collective-permute-start.12) | collective-permute-done | bytes 245792 | tf_op jit(solution)/shard_map/ppermute | solution.py:279
  69.9 2.6 %collective-permute-start.13 = (f32[1200,128]{1,0:T(8,128)S(1)}, f32[1200,128]{1,0:T(8,128)S(1)}, u32[]{:S(2)}, u32[]{:S(2)}) collective-permute-start(f32[1200,128]{1,0:T(8,128)S(1)} %slice.276), channel_id=1, source_target_pairs={{0,32},{32,0},{64,96},{96,64},{128,160},{160,128},{192,224},{224,1... | collective-permute-start | bytes 1843208 | tf_op jit(solution)/shard_map/ppermute | solution.py:271
  72.7 1.9 %collective-permute-done.22 = f32[576,128]{1,0:T(8,128)S(1)} collective-permute-done((f32[576,128]{1,0:T(8,128)S(1)}, f32[576,128]{1,0:T(8,128)S(1)}, u32[]{:S(2)}, u32[]{:S(2)}) %collective-permute-start.22) | collective-permute-done | bytes 294944 | tf_op jit(solution)/shard_map/ppermute | solution.py:271
  74.7 2.2 %collective-permute-start.23 = (f32[144,128]{1,0:T(8,128)S(1)}, f32[144,128]{1,0:T(8,128)S(1)}, u32[]{:S(2)}, u32[]{:S(2)}) collective-permute-start(f32[144,128]{1,0:T(8,128)S(1)} %slice.372), channel_id=1, source_target_pairs={{0,64},{32,224},{64,128},{96,32},{128,192},{160,96},{192,0},{224,1... | collective-permute-start | bytes 221192 | tf_op jit(solution)/shard_map/ppermute | solution.py:275
  78.3 4.2 %collective-permute-done.14 = f32[480,128]{1,0:T(8,128)S(1)} collective-permute-done((f32[480,128]{1,0:T(8,128)S(1)}, f32[480,128]{1,0:T(8,128)S(1)}, u32[]{:S(2)}, u32[]{:S(2)}) %collective-permute-start.14) | collective-permute-done | bytes 245792 | tf_op jit(solution)/shard_map/ppermute | solution.py:279
  84.4 3.3 %collective-permute-done.24 = f32[288,128]{1,0:T(8,128)S(1)} collective-permute-done((f32[288,128]{1,0:T(8,128)S(1)}, f32[288,128]{1,0:T(8,128)S(1)}, u32[]{:S(2)}, u32[]{:S(2)}) %collective-permute-start.24) | collective-permute-done | bytes 147488 | tf_op jit(solution)/shard_map/ppermute | solution.py:275
  87.7 2.9 %collective-permute-start.25 = (f32[144,128]{1,0:T(8,128)S(1)}, f32[144,128]{1,0:T(8,128)S(1)}, u32[]{:S(2)}, u32[]{:S(2)}) collective-permute-start(f32[144,128]{1,0:T(8,128)S(1)} %slice.375), channel_id=1, source_target_pairs={{0,32},{32,0},{64,96},{96,64},{128,160},{160,128},{192,224},{224,1... | collective-permute-start | bytes 221192 | tf_op jit(solution)/shard_map/ppermute | solution.py:271
  93.1 3.3 %collective-permute-start.26 = (f32[6,4,8,128]{3,0,2,1:T(8,128)S(1)}, f32[6,4,8,128]{3,0,2,1:T(8,128)S(1)}, u32[]{:S(2)}, u32[]{:S(2)}) collective-permute-start(f32[6,4,8,128]{3,0,2,1:T(8,128)S(1)} %get-tuple-element.41), channel_id=1, source_target_pairs={{32,64},{64,32},{96,128},{128,96},{160,192},{192,160},{33,65},{65,... | collective-permute-start | bytes 294920 | tf_op jit(solution)/shard_map/ppermute | solution.py:404
  96.4 2.9 %collective-permute-done.26 = f32[6,4,8,128]{3,0,2,1:T(8,128)S(1)} collective-permute-done((f32[6,4,8,128]{3,0,2,1:T(8,128)S(1)}, f32[6,4,8,128]{3,0,2,1:T(8,128)S(1)}, u32[]{:S(2)}, u32[]{:S(2)}) %collective-permute-start.26) | collective-permute-done | bytes 98336 | tf_op jit(solution)/shard_map/ppermute | solution.py:404
  99.8 1.3 %collective-permute-done.28 = f32[6,8,4,128]{3,0,2,1:T(8,128)S(1)} collective-permute-done((f32[6,8,4,128]{3,0,2,1:T(8,128)S(1)}, f32[6,8,4,128]{3,0,2,1:T(8,128)S(1)}, u32[]{:S(2)}, u32[]{:S(2)}) %collective-permute-start.28) | collective-permute-done | bytes 98336 | tf_op jit(solution)/shard_map/ppermute | solution.py:271
  102.5 5.8 %collective-permute-done.29 = f32[2,6,8,4,128]{4,1,3,2,0:T(8,128)S(1)} collective-permute-done((f32[2,6,8,4,128]{4,1,3,2,0:T(8,128)S(1)}, f32[2,6,8,4,128]{4,1,3,2,0:T(8,128)S(1)}, u32[]{:S(2)}, u32[]{:S(2)}) %collective-permute-start.29) | collective-permute-done | bytes 196640 | tf_op jit(solution)/shard_map/ppermute | solution.py:320
  108.4 1.3 %collective-permute-done.30 = f32[6,8,4,128]{3,0,2,1:T(8,128)S(1)} collective-permute-done((f32[6,8,4,128]{3,0,2,1:T(8,128)S(1)}, f32[6,8,4,128]{3,0,2,1:T(8,128)S(1)}, u32[]{:S(2)}, u32[]{:S(2)}) %collective-permute-start.30) | collective-permute-done | bytes 98336 | tf_op jit(solution)/shard_map/ppermute | solution.py:271
  111.8 1.3 %collective-permute-start.32 = (f32[2,4,384]{2,1,0:T(4,128)S(1)}, f32[2,4,384]{2,1,0:T(4,128)S(1)}, u32[]{:S(2)}, u32[]{:S(2)}) collective-permute-start(f32[2,4,384]{2,1,0:T(4,128)S(1)} %pad_maximum_fusion.12), channel_id=1, source_target_pairs={{0,1},{1,2},{2,3},{33,32},{34,33},{35,34},{64,65},{65,66},{66,67},... | collective-permute-start | bytes 36872 | tf_op jit(solution)/shard_map/ppermute | solution.py:320
  113.8 2.5 %collective-permute-done.32 = f32[2,4,384]{2,1,0:T(4,128)S(1)} collective-permute-done((f32[2,4,384]{2,1,0:T(4,128)S(1)}, f32[2,4,384]{2,1,0:T(4,128)S(1)}, u32[]{:S(2)}, u32[]{:S(2)}) %collective-permute-start.32) | collective-permute-done | bytes 12320 | tf_op jit(solution)/shard_map/ppermute | solution.py:320
  (118 shorter events, 23.7 us)
Async XLA Ops:
  15.5 4.5 %collective-permute-start = (f32[576,128]{1,0:T(8,128)S(1)}, f32[576,128]{1,0:T(8,128)S(1)}, u32[]{:S(2)}, u32[]{:S(2)}) collective-permute-start(f32[576,128]{1,0:T(8,128)S(1)} %slice.333), channel_id=1, source_target_pairs={{0,32},{32,0},{64,96},{96,64},{128,160},{160,128},{192,224},{224,1... | collective-permute-start | bytes 884744 | tf_op jit(solution)/shard_map/ppermute | solution.py:271
  22.4 7.0 %collective-permute-start.8 = (f32[720,128]{1,0:T(8,128)S(1)}, f32[720,128]{1,0:T(8,128)S(1)}, u32[]{:S(2)}, u32[]{:S(2)}) collective-permute-start(f32[720,128]{1,0:T(8,128)S(1)} %slice_add_fusion.11), channel_id=1, source_target_pairs={{0,64},{32,224},{64,128},{96,32},{128,192},{160,96},{192,0},{224,1... | collective-permute-start | bytes 1105928 | tf_op jit(solution)/shard_map/ppermute | solution.py:275
  24.8 19.7 %collective-permute-start.17 = (f32[2880,128]{1,0:T(8,128)S(1)}, f32[2880,128]{1,0:T(8,128)S(1)}, u32[]{:S(2)}, u32[]{:S(2)}) collective-permute-start(f32[2880,128]{1,0:T(8,128)S(1)} %slice.361), channel_id=1, source_target_pairs={{0,32},{32,0},{64,96},{96,64},{128,160},{160,128},{192,224},{224,1... | collective-permute-start | bytes 4423688 | tf_op jit(solution)/shard_map/ppermute | solution.py:271
  25.3 7.6 %collective-permute-start.18 = (f32[576,128]{1,0:T(8,128)S(1)}, f32[576,128]{1,0:T(8,128)S(1)}, u32[]{:S(2)}, u32[]{:S(2)}) collective-permute-start(f32[576,128]{1,0:T(8,128)S(1)} %slice_add_fusion.14), channel_id=1, source_target_pairs={{0,4},{4,8},{8,12},{12,16},{16,20},{20,24},{24,28},{28,0},{32,60},... | collective-permute-start | bytes 884744 | tf_op jit(solution)/shard_map/ppermute | solution.py:279
  29.3 19.4 %collective-permute-start.5 = (f32[4320,128]{1,0:T(8,128)S(1)}, f32[4320,128]{1,0:T(8,128)S(1)}, u32[]{:S(2)}, u32[]{:S(2)}) collective-permute-start(f32[4320,128]{1,0:T(8,128)S(1)} %slice.329), channel_id=1, source_target_pairs={{0,32},{32,0},{64,96},{96,64},{128,160},{160,128},{192,224},{224,1... | collective-permute-start | bytes 6635528 | tf_op jit(solution)/shard_map/ppermute | solution.py:271
  29.5 10.8 %collective-permute-start.9 = (f32[1440,128]{1,0:T(8,128)S(1)}, f32[1440,128]{1,0:T(8,128)S(1)}, u32[]{:S(2)}, u32[]{:S(2)}) collective-permute-start(f32[1440,128]{1,0:T(8,128)S(1)} %pad_maximum_fusion.1), channel_id=1, source_target_pairs={{0,64},{32,224},{64,128},{96,32},{128,192},{160,96},{192,0},{224,1... | collective-permute-start | bytes 2211848 | tf_op jit(solution)/shard_map/ppermute | solution.py:275
  31.9 18.1 %collective-permute-start.6 = (f32[1200,128]{1,0:T(8,128)S(1)}, f32[1200,128]{1,0:T(8,128)S(1)}, u32[]{:S(2)}, u32[]{:S(2)}) collective-permute-start(f32[1200,128]{1,0:T(8,128)S(1)} %slice_add_fusion.5), channel_id=1, source_target_pairs={{0,64},{32,224},{64,128},{96,32},{128,192},{160,96},{192,0},{224,1... | collective-permute-start | bytes 1843208 | tf_op jit(solution)/shard_map/ppermute | solution.py:275
  33.0 11.6 %collective-permute-start.19 = (f32[1152,128]{1,0:T(8,128)S(1)}, f32[1152,128]{1,0:T(8,128)S(1)}, u32[]{:S(2)}, u32[]{:S(2)}) collective-permute-start(f32[1152,128]{1,0:T(8,128)S(1)} %pad_maximum_fusion.2), channel_id=1, source_target_pairs={{0,4},{4,8},{8,12},{12,16},{16,20},{20,24},{24,28},{28,0},{32,60},... | collective-permute-start | bytes 1769480 | tf_op jit(solution)/shard_map/ppermute | solution.py:279
  40.3 8.7 %collective-permute-start.10 = (f32[720,128]{1,0:T(8,128)S(1)}, f32[720,128]{1,0:T(8,128)S(1)}, u32[]{:S(2)}, u32[]{:S(2)}) collective-permute-start(f32[720,128]{1,0:T(8,128)S(1)} %slice.349), channel_id=1, source_target_pairs={{0,32},{32,0},{64,96},{96,64},{128,160},{160,128},{192,224},{224,1... | collective-permute-start | bytes 1105928 | tf_op jit(solution)/shard_map/ppermute | solution.py:271
  44.7 12.1 %collective-permute-start.20 = (f32[1152,128]{1,0:T(8,128)S(1)}, f32[1152,128]{1,0:T(8,128)S(1)}, u32[]{:S(2)}, u32[]{:S(2)}) collective-permute-start(f32[1152,128]{1,0:T(8,128)S(1)} %slice_add_fusion.6), channel_id=1, source_target_pairs={{0,4},{4,8},{8,12},{12,16},{16,20},{20,24},{24,28},{28,0},{32,60},... | collective-permute-start | bytes 1769480 | tf_op jit(solution)/shard_map/ppermute | solution.py:279
  49.1 7.7 %collective-permute-start.11 = (f32[240,128]{1,0:T(8,128)S(1)}, f32[240,128]{1,0:T(8,128)S(1)}, u32[]{:S(2)}, u32[]{:S(2)}) collective-permute-start(f32[240,128]{1,0:T(8,128)S(1)} %slice.351), channel_id=1, source_target_pairs={{0,4},{4,8},{8,12},{12,16},{16,20},{20,24},{24,28},{28,0},{32,60},... | collective-permute-start | bytes 368648 | tf_op jit(solution)/shard_map/ppermute | solution.py:279
  50.2 19.7 %collective-permute-start.7 = (f32[2400,128]{1,0:T(8,128)S(1)}, f32[2400,128]{1,0:T(8,128)S(1)}, u32[]{:S(2)}, u32[]{:S(2)}) collective-permute-start(f32[2400,128]{1,0:T(8,128)S(1)} %pad_maximum_fusion), channel_id=1, source_target_pairs={{0,64},{32,224},{64,128},{96,32},{128,192},{160,96},{192,0},{224,1... | collective-permute-start | bytes 3686408 | tf_op jit(solution)/shard_map/ppermute | solution.py:275
  56.9 15.6 %collective-permute-start.21 = (f32[1152,128]{1,0:T(8,128)S(1)}, f32[1152,128]{1,0:T(8,128)S(1)}, u32[]{:S(2)}, u32[]{:S(2)}) collective-permute-start(f32[1152,128]{1,0:T(8,128)S(1)} %slice_add_fusion.7), channel_id=1, source_target_pairs={{0,4},{4,8},{8,12},{12,16},{16,20},{20,24},{24,28},{28,0},{32,60},... | collective-permute-start | bytes 1769480 | tf_op jit(solution)/shard_map/ppermute | solution.py:279
  60.4 9.5 %collective-permute-start.12 = (f32[480,128]{1,0:T(8,128)S(1)}, f32[480,128]{1,0:T(8,128)S(1)}, u32[]{:S(2)}, u32[]{:S(2)}) collective-permute-start(f32[480,128]{1,0:T(8,128)S(1)} %pad_maximum_fusion.10), channel_id=1, source_target_pairs={{0,4},{4,8},{8,12},{12,16},{16,20},{20,24},{24,28},{28,0},{32,60},... | collective-permute-start | bytes 737288 | tf_op jit(solution)/shard_map/ppermute | solution.py:279
  69.9 7.0 %collective-permute-start.13 = (f32[1200,128]{1,0:T(8,128)S(1)}, f32[1200,128]{1,0:T(8,128)S(1)}, u32[]{:S(2)}, u32[]{:S(2)}) collective-permute-start(f32[1200,128]{1,0:T(8,128)S(1)} %slice.276), channel_id=1, source_target_pairs={{0,32},{32,0},{64,96},{96,64},{128,160},{160,128},{192,224},{224,1... | collective-permute-start | bytes 1843208 | tf_op jit(solution)/shard_map/ppermute | solution.py:271
  74.7 3.6 %collective-permute-start.23 = (f32[144,128]{1,0:T(8,128)S(1)}, f32[144,128]{1,0:T(8,128)S(1)}, u32[]{:S(2)}, u32[]{:S(2)}) collective-permute-start(f32[144,128]{1,0:T(8,128)S(1)} %slice.372), channel_id=1, source_target_pairs={{0,64},{32,224},{64,128},{96,32},{128,192},{160,96},{192,0},{224,1... | collective-permute-start | bytes 221192 | tf_op jit(solution)/shard_map/ppermute | solution.py:275
  77.1 5.4 %collective-permute-start.14 = (f32[480,128]{1,0:T(8,128)S(1)}, f32[480,128]{1,0:T(8,128)S(1)}, u32[]{:S(2)}, u32[]{:S(2)}) collective-permute-start(f32[480,128]{1,0:T(8,128)S(1)} %maximum_add_fusion.1), channel_id=1, source_target_pairs={{0,4},{4,8},{8,12},{12,16},{16,20},{20,24},{24,28},{28,0},{32,60},... | collective-permute-start | bytes 737288 | tf_op jit(solution)/shard_map/ppermute | solution.py:279
  82.6 8.0 %collective-permute-start.15 = (f32[480,128]{1,0:T(8,128)S(1)}, f32[480,128]{1,0:T(8,128)S(1)}, u32[]{:S(2)}, u32[]{:S(2)}) collective-permute-start(f32[480,128]{1,0:T(8,128)S(1)} %maximum_add_fusion), channel_id=1, source_target_pairs={{0,4},{4,8},{8,12},{12,16},{16,20},{20,24},{24,28},{28,0},{32,60},... | collective-permute-start | bytes 737288 | tf_op jit(solution)/shard_map/ppermute | solution.py:279
  83.6 4.1 %collective-permute-start.24 = (f32[288,128]{1,0:T(8,128)S(1)}, f32[288,128]{1,0:T(8,128)S(1)}, u32[]{:S(2)}, u32[]{:S(2)}) collective-permute-start(f32[288,128]{1,0:T(8,128)S(1)} %pad_maximum_fusion.11), channel_id=1, source_target_pairs={{0,64},{32,224},{64,128},{96,32},{128,192},{160,96},{192,0},{224,1... | collective-permute-start | bytes 442376 | tf_op jit(solution)/shard_map/ppermute | solution.py:275
  87.7 3.9 %collective-permute-start.25 = (f32[144,128]{1,0:T(8,128)S(1)}, f32[144,128]{1,0:T(8,128)S(1)}, u32[]{:S(2)}, u32[]{:S(2)}) collective-permute-start(f32[144,128]{1,0:T(8,128)S(1)} %slice.375), channel_id=1, source_target_pairs={{0,32},{32,0},{64,96},{96,64},{128,160},{160,128},{192,224},{224,1... | collective-permute-start | bytes 221192 | tf_op jit(solution)/shard_map/ppermute | solution.py:271
  92.6 3.8 %collective-permute-start.27 = (f32[6,4,8,128]{3,0,2,1:T(8,128)S(1)}, f32[6,4,8,128]{3,0,2,1:T(8,128)S(1)}, u32[]{:S(2)}, u32[]{:S(2)}) collective-permute-start(f32[6,4,8,128]{3,0,2,1:T(8,128)S(1)} %get-tuple-element.40), channel_id=1, source_target_pairs={{0,32},{32,0},{64,96},{96,64},{128,160},{160,128},{192,224},{224,1... | collective-permute-start | bytes 294920 | tf_op jit(solution)/shard_map/ppermute | solution.py:271
  93.1 6.3 %collective-permute-start.26 = (f32[6,4,8,128]{3,0,2,1:T(8,128)S(1)}, f32[6,4,8,128]{3,0,2,1:T(8,128)S(1)}, u32[]{:S(2)}, u32[]{:S(2)}) collective-permute-start(f32[6,4,8,128]{3,0,2,1:T(8,128)S(1)} %get-tuple-element.41), channel_id=1, source_target_pairs={{32,64},{64,32},{96,128},{128,96},{160,192},{192,160},{33,65},{65,... | collective-permute-start | bytes 294920 | tf_op jit(solution)/shard_map/ppermute | solution.py:404
  101.2 7.1 %collective-permute-start.29 = (f32[2,6,8,4,128]{4,1,3,2,0:T(8,128)S(1)}, f32[2,6,8,4,128]{4,1,3,2,0:T(8,128)S(1)}, u32[]{:S(2)}, u32[]{:S(2)}) collective-permute-start(f32[2,6,8,4,128]{4,1,3,2,0:T(8,128)S(1)} %pad_maximum_fusion.9), channel_id=1, source_target_pairs={{0,4},{4,8},{8,12},{12,16},{16,20},{20,24},{24,28},{36,32},{40,36}... | collective-permute-start | bytes 589832 | tf_op jit(solution)/shard_map/ppermute | solution.py:320
  111.8 4.5 %collective-permute-start.32 = (f32[2,4,384]{2,1,0:T(4,128)S(1)}, f32[2,4,384]{2,1,0:T(4,128)S(1)}, u32[]{:S(2)}, u32[]{:S(2)}) collective-permute-start(f32[2,4,384]{2,1,0:T(4,128)S(1)} %pad_maximum_fusion.12), channel_id=1, source_target_pairs={{0,1},{1,2},{2,3},{33,32},{34,33},{35,34},{64,65},{65,66},{66,67},... | collective-permute-start | bytes 36872 | tf_op jit(solution)/shard_map/ppermute | solution.py:320
  (13 other events, 70.3 us)
